TPU v7x, 32 devices: a whole 2x2x4 slice. The times are simulated.
32 devices in a mesh: dp: 2 (over x), seq: 2 (over core), expert: 8 (over z, y).
Axes of the slice: x: 2, y: 2, z: 4, core: 2. Of those that a mesh axis runs over, the one named last changes fastest.
Arguments:
- out_grad: bfloat16 [4096, 2048], P(('dp', 'seq', 'expert')), may hold values from -6 to 6
- saved_act: bfloat16 [4096, 8, 768], P(('dp', 'seq', 'expert')), may hold values from -0.29882812 to 0.29882812
- gate_probs: float32 [4096, 8], P(('dp', 'seq', 'expert')), may hold values from 0.02 to 0.6
- routes: int32 [4096, 8], P(('dp', 'seq', 'expert')), may hold values from 0 to 15, all different within a row; in each aligned block of 128 rows (0 to 127, 128 to 255, ...) at most 72 rows name the same one
- w_down: bfloat16 [16, 768, 2048], P(('seq', 'expert'), 'dp'), may hold values from -0.21875 to 0.21875
Outputs:
- act_grad: bfloat16 [4096, 8, 768], P(('dp', 'seq', 'expert'))
- prob_grad: float32 [4096, 8], P(('dp', 'seq', 'expert'))
- weight_grad: bfloat16 [16, 768, 2048], P(('seq', 'expert'), 'dp')
Inputs may be any that keep to these rules, and one draw needn't show every extreme that they name: `routes`: within the rows of one device (aligned blocks of 128 tokens) no expert is named by more than 72 tokens, a bound that some block reaches; each token names 8 different experts.
All inputs are finite; a program needn't handle non-finite values.
Results may differ from a plain program's by a relative error of at most 0.014.
Values may be sent and summed in bfloat16 or wider, within the bound.
A program may use at most 128 MiB of HBM per device.

v0:
```python
import jax
import jax.numpy as jnp
from jax import lax
from jax.sharding import PartitionSpec as P


def local(out_grad, saved_act, gate_probs, routes, w_down):
    token_count = routes.shape[0]
    top_count = routes.shape[1]
    hidden_width = saved_act.shape[2]
    feature_width = out_grad.shape[1]
    owners = lax.axis_size(("seq", "expert"))
    pair_count = token_count * top_count
    most_rows = max(2, min(token_count, pair_count // owners + pair_count // (8 * owners)))
    capacity = owners * most_rows
    expert_of = routes.reshape(pair_count)
    one_hot = (expert_of[:, None] == jnp.arange(owners, dtype=jnp.int32)[None, :]).astype(jnp.int32)
    rank_of = jnp.sum((jnp.cumsum(one_hot, axis=0) - one_hot) * one_hot, axis=1)
    slot_of = expert_of * most_rows + rank_of
    source_row = (
        jnp.zeros((capacity,), jnp.int32).at[slot_of].set(jnp.arange(pair_count, dtype=jnp.int32))
    )
    prob_rows = jnp.zeros((capacity,), jnp.float32).at[slot_of].set(gate_probs.reshape(pair_count))
    grad_rows = jnp.take(out_grad, source_row // top_count, axis=0)
    act_rows = jnp.take(saved_act.reshape(pair_count, hidden_width), source_row, axis=0)
    send_grad = grad_rows.reshape(owners, most_rows * feature_width)
    send_act = act_rows.reshape(owners, most_rows * hidden_width)
    send_prob = prob_rows.reshape(owners, most_rows)
    arrived = (
        lax.all_to_all(send_grad, ("seq", "expert"), split_axis=0, concat_axis=0, tiled=True),
        lax.all_to_all(send_act, ("seq", "expert"), split_axis=0, concat_axis=0, tiled=True),
        lax.all_to_all(
            send_prob.astype(jnp.bfloat16),
            ("seq", "expert"),
            split_axis=0,
            concat_axis=0,
            tiled=True,
        ).astype(send_prob.dtype),
    )
    recv_grad = arrived[0].reshape(capacity, feature_width)
    recv_act = arrived[1].reshape(capacity, hidden_width)
    recv_prob = arrived[2].reshape(capacity)
    expert_grad = lax.dot_general(
        recv_grad,
        lax.all_gather(w_down, "dp", axis=1, tiled=True)[0],
        (((1,), (1,)), ((), ())),
        preferred_element_type=jnp.float32,
    )
    act_back = (recv_prob[:, None] * expert_grad).astype(jnp.bfloat16)
    prob_back = jnp.sum(recv_act.astype(jnp.float32) * expert_grad, axis=1)
    scaled = (recv_prob[:, None] * recv_grad.astype(jnp.float32)).astype(jnp.bfloat16)
    weight_part = lax.psum_scatter(
        lax.dot_general(
            recv_act, scaled, (((0,), (0,)), ((), ())), preferred_element_type=jnp.float32
        ).astype(jnp.bfloat16),
        "dp",
        scatter_dimension=0,
        tiled=True,
    )
    weight_grad = weight_part.reshape(w_down.shape)
    back_act = act_back.reshape(owners, most_rows * hidden_width)
    back_prob = prob_back.reshape(owners, most_rows)
    returned = (
        lax.all_to_all(back_act, ("seq", "expert"), split_axis=0, concat_axis=0, tiled=True),
        lax.all_to_all(
            back_prob.astype(jnp.bfloat16),
            ("seq", "expert"),
            split_axis=0,
            concat_axis=0,
            tiled=True,
        ).astype(back_prob.dtype),
    )
    slot_grad = returned[0].reshape(capacity, hidden_width)
    slot_prob = returned[1].reshape(capacity)
    act_grad = jnp.take(slot_grad, slot_of, axis=0).reshape(token_count, top_count, hidden_width)
    prob_grad = jnp.take(slot_prob, slot_of, axis=0).reshape(token_count, top_count)
    return (act_grad, prob_grad, weight_grad)


def solution(mesh):
    in_specs = (
        P(("dp", "seq", "expert"), None),
        P(("dp", "seq", "expert"), None, None),
        P(("dp", "seq", "expert"), None),
        P(("dp", "seq", "expert"), None),
        P(("seq", "expert"), "dp", None),
    )
    out_specs = (
        P(("dp", "seq", "expert"), None, None),
        P(("dp", "seq", "expert"), None),
        P(("seq", "expert"), "dp", None),
    )
    return jax.shard_map(local, mesh=mesh, in_specs=in_specs, out_specs=out_specs, check_vma=False)
```

profile of v0, /device:TPU:0, one launch (start us, length us, event | category | flops | bytes accessed | tf_op | source)
XLA Modules:
  0.0 490.6 jit_solution(15474529246030302256)
XLA Ops:
  8.3 4.5 reduce-window.6
  14.3 4.3 scatter_custom_fusion
  19.3 7.4 %all-to-all-start = ((bf16[16,1,72]{2,1,0:T(2,128)(2,1)}), bf16[16,1,72]{2,1,0:T(2,128)(2,1)S(1)}, u32[]{:S(2)}, u32[]{:S(2)}) async-start(bf16[16,1,72]{2,1,0:T(2,128)(2,1)} %convert_element_type.104), calls=%async_computation | async-start | bytes 16384 | tf_op jit(solution)/shard_map/all_to_all | solution.py:32
  33.2 4.6 gather_fusion.2
  41.3 6.0 %gather_fusion = bf16[1152,2048]{1,0:T(8,128)(2,1)} fusion(bf16[128,2048]{1,0:T(8,128)(2,1)S(1)} %copy-done.2, s32[2048]{0:T(1024)S(1)} %pad_clamp_fusion.1), kind=kCustom, calls=%fused_computation | custom fusion | bytes 9441792 | tf_op jit(solution)/shard_map/jit(_take)/gather | solution.py:24
  47.3 5.2 %gather.25 = bf16[16,1,147456]{2,0,1:T(8,128)(2,1)} reshape(bf16[1152,2048]{1,0:T(8,128)(2,1)} %gather_fusion) | data formatting | bytes 9437184 | tf_op jit(solution)/shard_map/jit(_take)/gather | solution.py:24
  54.7 4.7 broadcast_in_dim.62
  66.3 6.5 %all-to-all-start.3 = ((bf16[16,2,27648]{2,1,0:T(2,128)(2,1)}), bf16[16,2,27648]{2,1,0:T(2,128)(2,1)S(1)}, u32[]{:S(2)}, u32[]{:S(2)}) async-start(bf16[16,2,27648]{2,1,0:T(2,128)(2,1)} %reshape.299), calls=%async_computation.3 | async-start | bytes 3538944 | tf_op jit(solution)/shard_map/all_to_all | solution.py:31
  72.8 4.8 broadcast_select_fusion
  77.6 6.8 %reduce.15 = bf16[16,147456]{1,0:T(8,128)(2,1)} reduce(bf16[16,1,147456]{2,0,1:T(8,128)(2,1)} %broadcast_select_fusion, bf16[]{:T(256)} %broadcast.127), dimensions={1}, to_apply=%copy.40.reduce_sub_computation | reduce | bytes 9437186 | tf_op jit(solution)/shard_map/jit(_take)/select_n | solution.py:24
  84.4 7.3 %reshape.295 = bf16[16,2,73728]{2,1,0:T(2,128)(2,1)} reshape(bf16[16,147456]{1,0:T(8,128)(2,1)} %reduce.15) | data formatting | bytes 9437184
  91.7 22.0 %all-to-all-done.3 = bf16[16,2,27648]{2,1,0:T(2,128)(2,1)S(1)} async-done(((bf16[16,2,27648]{2,1,0:T(2,128)(2,1)}), bf16[16,2,27648]{2,1,0:T(2,128)(2,1)S(1)}, u32[]{:S(2)}, u32[]{:S(2)}) %all-to-all-start.3) | async-done | bytes 1769504 | tf_op jit(solution)/shard_map/all_to_all | solution.py:31
  113.7 4.6 all-to-all-start.1
  119.2 4.3 mul.56
  123.5 17.7 %mul.57 = f32[16,1,147456]{2,1,0:T(1,128)} reshape(f32[16,72,2048]{2,1,0:T(8,128)} %mul.56) | data formatting | bytes 18874368 | tf_op jit(solution)/shard_map/mul | solution.py:51
  141.2 6.3 %reshape.300 = bf16[16,1,55296]{2,1,0:T(2,128)(2,1)} reshape(bf16[16,2,27648]{2,1,0:T(2,128)(2,1)S(1)} %all-to-all-done.3) | data formatting | bytes 3538944
  147.5 39.0 %reduce.3 = bf16[16,55296]{1,0:T(8,128)(2,1)} reduce(bf16[16,1,55296]{2,1,0:T(2,128)(2,1)} %reshape.300, bf16[]{:T(256)} %constant.87), dimensions={1}, to_apply=%all_to_all.26.reduce_sub_computation | reduce | bytes 3538946 | tf_op jit(solution)/shard_map/all_to_all | solution.py:31
  188.6 30.1 %all-to-all-done.1 = bf16[16,2,73728]{2,1,0:T(2,128)(2,1)} async-done(((bf16[16,2,73728]{2,1,0:T(2,128)(2,1)}), bf16[16,2,73728]{2,1,0:T(2,128)(2,1)}, u32[]{:S(2)}, u32[]{:S(2)}) %all-to-all-start.1) | async-done | bytes 4718624 | tf_op jit(solution)/shard_map/all_to_all | solution.py:30
  218.7 12.8 %reshape.296 = bf16[16,1,147456]{2,1,0:T(2,128)(2,1)} reshape(bf16[16,2,73728]{2,1,0:T(2,128)(2,1)} %all-to-all-done.1) | data formatting | bytes 9437184
  231.5 62.7 %convert_reduce_fusion = (bf16[16,147456]{1,0:T(8,128)(2,1)}, bf16[16,147456]{1,0:T(8,128)(2,1)}) fusion(f32[16,1,147456]{2,1,0:T(1,128)} %mul.57, bf16[16,1,147456]{2,1,0:T(2,128)(2,1)} %reshape.296), kind=kLoop, calls=%fused_computation.6 | loop fusion | flops 7077888 | bytes 23592960 | tf_op jit(solution)/shard_map/convert_element_type | solution.py:51
  294.3 5.3 %convert_element_type.99 = bf16[1152,2048]{1,0:T(8,128)(2,1)} reshape(bf16[16,147456]{1,0:T(8,128)(2,1)} %get-tuple-element.12) | data formatting | bytes 9437184 | tf_op jit(solution)/shard_map/convert_element_type | solution.py:51
  299.6 8.1 %convolution_convert_fusion = bf16[768,2048]{1,0:T(8,128)(2,1)} fusion(bf16[1152,768]{1,0:T(8,128)(2,1)S(1)} %reshape.220, bf16[1152,2048]{1,0:T(8,128)(2,1)} %convert_element_type.99), kind=kOutput, calls=%fused_computation.9 | convolution fusion | flops 3625451520 | bytes 9633792 | tf_op jit(solution)/shard_map/dot_general | solution.py:53
  310.0 5.3 %reshape.217 = bf16[1152,2048]{1,0:T(8,128)(2,1)} reshape(bf16[16,147456]{1,0:T(8,128)(2,1)} %get-tuple-element.13) | data formatting | bytes 9437184 | tf_op jit(solution)/shard_map/reshape | solution.py:40
  315.4 9.8 %multiply_reduce_fusion = (bf16[1152]{0:T(1024)(128)(2,1)S(1)}, bf16[1152,768]{0,1:T(8,128)(2,1)}) fusion(bf16[1152,768]{0,1:T(8,128)(2,1)S(1)} %copy-done.4, f32[1152]{0:T(1024)S(1)} %reshape.222, bf16[1152,2048]{1,0:T(8,128)(2,1)} %reshape.217, bf16[1,768,2048]{2,1,0:T(8,128)(2,1)} %all-gather.2.cloned.1.call-done), kind=kOutput, calls=%fused_computation.7 | convolution fusion | flops 3628301312 | bytes 11410176 | tf_op jit(solution)/shard_map/dot_general | solution.py:43
  325.9 7.9 %all-to-all-start.4 = ((bf16[16,1,72]{2,1,0:T(2,128)(2,1)}), bf16[16,1,72]{2,1,0:T(2,128)(2,1)S(1)}, u32[]{:S(2)}, u32[]{:S(2)}) async-start(bf16[16,1,72]{2,1,0:T(2,128)(2,1)} %convert_element_type.105), calls=%async_computation.4 | async-start | bytes 16384 | tf_op jit(solution)/shard_map/all_to_all | solution.py:65
  340.0 38.5 %reduce.16 = bf16[16,55296]{1,0:T(8,128)(2,1)S(1)} reduce(bf16[16,1,55296]{2,1,0:T(2,128)(2,1)} %all_to_all.28, bf16[]{:T(256)} %broadcast.127), dimensions={1}, to_apply=%all_to_all.28.reduce_sub_computation | reduce | bytes 3538946 | tf_op jit(solution)/shard_map/all_to_all | solution.py:64
  380.9 6.4 %all-to-all-start.2 = ((bf16[16,2,27648]{2,1,0:T(2,128)(2,1)}), bf16[16,2,27648]{2,1,0:T(2,128)(2,1)S(1)}, u32[]{:S(2)}, u32[]{:S(2)}) async-start(bf16[16,2,27648]{2,1,0:T(2,128)(2,1)} %reshape.297), calls=%async_computation.2 | async-start | bytes 3538944 | tf_op jit(solution)/shard_map/all_to_all | solution.py:64
  387.5 6.2 %gather_fusion.3 = f32[1024]{0:T(1024)S(1)} fusion(f32[1152]{0:T(1024)S(1)} %reshape.223, s32[1024]{0:T(1024)S(1)} %broadcast_clamp_fusion), kind=kCustom, calls=%fused_computation.3 | custom fusion | bytes 12288 | tf_op jit(solution)/shard_map/jit(_take)/gather | solution.py:76
  394.4 33.8 %all-to-all-done.2 = bf16[16,2,27648]{2,1,0:T(2,128)(2,1)S(1)} async-done(((bf16[16,2,27648]{2,1,0:T(2,128)(2,1)}), bf16[16,2,27648]{2,1,0:T(2,128)(2,1)S(1)}, u32[]{:S(2)}, u32[]{:S(2)}) %all-to-all-start.2) | async-done | bytes 1769504 | tf_op jit(solution)/shard_map/all_to_all | solution.py:64
  428.2 6.2 %reshape.298 = bf16[16,1,55296]{2,1,0:T(2,128)(2,1)} reshape(bf16[16,2,27648]{2,1,0:T(2,128)(2,1)S(1)} %all-to-all-done.2) | data formatting | bytes 3538944
  434.5 39.0 %reduce.2 = bf16[16,55296]{1,0:T(8,128)(2,1)} reduce(bf16[16,1,55296]{2,1,0:T(2,128)(2,1)} %reshape.298, bf16[]{:T(256)} %constant.87), dimensions={1}, to_apply=%all_to_all.25.reduce_sub_computation | reduce | bytes 3538946 | tf_op jit(solution)/shard_map/all_to_all | solution.py:64
  475.5 5.2 %gather_fusion.1 = bf16[1024,768]{1,0:T(8,128)(2,1)} fusion(bf16[1152,768]{1,0:T(8,128)(2,1)S(1)} %reshape.218, s32[1024]{0:T(1024)S(1)} %broadcast_clamp_fusion), kind=kCustom, calls=%fused_computation.1 | custom fusion | bytes 3149824 | tf_op jit(solution)/shard_map/jit(_take)/gather | solution.py:75
  (70 shorter events, 42.4 us)
Async XLA Ops:
  7.2 26.0 %copy-start = (bf16[128,8,768]{2,1,0:T(8,128)(2,1)S(1)}, bf16[128,8,768]{2,1,0:T(8,128)(2,1)}, u32[]{:S(2)}) copy-start(bf16[128,8,768]{2,1,0:T(8,128)(2,1)} %param.6) | copy-start | bytes 4718596
  19.3 47.0 %all-to-all-start = ((bf16[16,1,72]{2,1,0:T(2,128)(2,1)}), bf16[16,1,72]{2,1,0:T(2,128)(2,1)S(1)}, u32[]{:S(2)}, u32[]{:S(2)}) async-start(bf16[16,1,72]{2,1,0:T(2,128)(2,1)} %convert_element_type.104), calls=%async_computation | async-start | bytes 16384 | tf_op jit(solution)/shard_map/all_to_all | solution.py:32
  37.8 1.8 copy-start.3
  37.8 3.5 copy-start.2
  66.3 47.4 %all-to-all-start.3 = ((bf16[16,2,27648]{2,1,0:T(2,128)(2,1)}), bf16[16,2,27648]{2,1,0:T(2,128)(2,1)S(1)}, u32[]{:S(2)}, u32[]{:S(2)}) async-start(bf16[16,2,27648]{2,1,0:T(2,128)(2,1)} %reshape.299), calls=%async_computation.3 | async-start | bytes 3538944 | tf_op jit(solution)/shard_map/all_to_all | solution.py:31
  113.7 105.0 %all-to-all-start.1 = ((bf16[16,2,73728]{2,1,0:T(2,128)(2,1)}), bf16[16,2,73728]{2,1,0:T(2,128)(2,1)}, u32[]{:S(2)}, u32[]{:S(2)}) async-start(bf16[16,2,73728]{2,1,0:T(2,128)(2,1)} %reshape.295), calls=%async_computation.1 | async-start | bytes 9437184 | tf_op jit(solution)/shard_map/all_to_all | solution.py:30
  118.4 197.0 %all-gather.2.cloned.1.call-start = ((), (), s32[]{:S(2)}) async-start(), calls=%async_computation.6 | async-start | bytes 4718592 | tf_op jit(solution)/shard_map/all_gather | solution.py:45
  119.1 364.4 %reduce-scatter.2.cloned.1.call-start = ((), (), s32[]{:S(2)}) async-start(), calls=%async_computation.7 | async-start | bytes 4718592 | tf_op jit(solution)/shard_map/reduce_scatter | solution.py:52
  310.0 5.3 %copy-start.4 = (bf16[1152,768]{0,1:T(8,128)(2,1)S(1)}, bf16[1152,768]{0,1:T(8,128)(2,1)}, u32[]{:S(2)}) copy-start(bf16[1152,768]{0,1:T(8,128)(2,1)} %copy.44) | copy-start | bytes 5308420
  325.9 55.0 %all-to-all-start.4 = ((bf16[16,1,72]{2,1,0:T(2,128)(2,1)}), bf16[16,1,72]{2,1,0:T(2,128)(2,1)S(1)}, u32[]{:S(2)}, u32[]{:S(2)}) async-start(bf16[16,1,72]{2,1,0:T(2,128)(2,1)} %convert_element_type.105), calls=%async_computation.4 | async-start | bytes 16384 | tf_op jit(solution)/shard_map/all_to_all | solution.py:65
  380.9 47.3 %all-to-all-start.2 = ((bf16[16,2,27648]{2,1,0:T(2,128)(2,1)}), bf16[16,2,27648]{2,1,0:T(2,128)(2,1)S(1)}, u32[]{:S(2)}, u32[]{:S(2)}) async-start(bf16[16,2,27648]{2,1,0:T(2,128)(2,1)} %reshape.297), calls=%async_computation.2 | async-start | bytes 3538944 | tf_op jit(solution)/shard_map/all_to_all | solution.py:64
  475.5 8.0 %copy-start.1 = (bf16[128,8,768]{2,1,0:T(8,128)(2,1)S(1)}, bf16[128,8,768]{2,1,0:T(8,128)(2,1)}, u32[]{:S(2)}) copy-start(bf16[128,8,768]{2,1,0:T(8,128)(2,1)} %param.6) | copy-start | bytes 4718596
Sparse Core Ops, SparseCore 0:
  120.8 46.1 all-gather.1
  307.8 47.1 reduce-scatter.1
where the time goes:
time: 500 us; the launch traced here: 491 us
  other arithmetic  203 us (41%)
  local copies, waits for them, and re-layouts  136 us (27%)
  waiting for transfers between devices  86.7 us (17%)
  starting transfers between devices  32.8 us (7%)
  matrix products  17.9 us (4%)
  between operations  14.6 us (3%)
    all_to_all x2, other arithmetic, local(): lax.all_to_all(back_act, ('seq', 'expert'), split_axis=0, concat_axis=0,...  77.5 us
    convert_element_type x1, other arithmetic, local(): (recv_prob[:, None] * recv_grad.astype(jnp.float32)).astype(jnp.bfloat16)  62.7 us
    unnamed x19, local copies, waits for them, and re-layouts  41.1 us
    all_to_all x1, other arithmetic, local(): lax.all_to_all(send_act, ('seq', 'expert'), split_axis=0, concat_axis=0,...  39 us
    all_to_all x1, waiting for transfers between devices, local(): lax.all_to_all(back_act, ('seq', 'expert'), split_axis=0, concat_axis=0,...  33.8 us
    all_to_all x1, waiting for transfers between devices, local(): lax.all_to_all(send_grad, ('seq', 'expert'), split_axis=0, concat_axis=0,...  30.1 us
    mul x2, local copies, waits for them, and re-layouts, local(): recv_prob[:, None] * recv_grad.astype(jnp.float32)  22 us
    all_to_all x1, waiting for transfers between devices, local(): lax.all_to_all(send_act, ('seq', 'expert'), split_axis=0, concat_axis=0,...  22 us
  transfers between devices with their start and end apart: 7, of which 3 were waited for; matrix products, arithmetic and copies ran while one was open for 69% of the time, Pallas kernels for 0%

commit v1 on v0

v1 whole, which is shorter than its diff:
```python
import jax
import jax.numpy as jnp
from jax import lax
from jax.sharding import PartitionSpec as P

GROUP = ("seq", "expert")


def local(out_grad, saved_act, gate_probs, routes, w_down):
    tokens, top = routes.shape
    hidden = saved_act.shape[2]
    features = out_grad.shape[1]
    owners = lax.axis_size(GROUP)
    pairs = tokens * top
    most = max(2, min(tokens, pairs // owners + pairs // (8 * owners)))
    rows = -(-most // 8) * 8
    capacity = owners * rows
    f32, bf16 = jnp.float32, jnp.bfloat16

    grads_all = lax.all_gather(out_grad, GROUP, axis=0)
    routes_all = lax.all_gather(routes, GROUP, axis=0)
    weight = lax.all_gather(w_down, "dp", axis=1, tiled=True)[0]

    ids = jnp.arange(owners, dtype=jnp.int32)
    named = routes[:, :, None] == ids[None, None, :]
    names = jnp.any(named, axis=1)
    before = (jnp.arange(tokens)[:, None] > jnp.arange(tokens)[None, :]).astype(bf16)
    rank = jnp.dot(before, names.astype(bf16), preferred_element_type=f32)
    rank_of = jnp.sum(jnp.where(named, rank[:, None, :], 0.0), axis=2).astype(jnp.int32)
    slot = (routes * rows + rank_of).reshape(pairs)
    place = (slot[:, None] == jnp.arange(capacity, dtype=jnp.int32)[None, :]).astype(bf16)

    act = saved_act.reshape(pairs, hidden)
    gate = gate_probs.reshape(pairs, 1)
    scaled = (act.astype(f32) * gate).astype(bf16)
    packed = lax.dot_general(
        place, scaled, (((0,), (0,)), ((), ())), preferred_element_type=f32
    ).astype(bf16)
    recv_act = lax.all_to_all(
        packed.reshape(owners, rows, hidden), GROUP, split_axis=0, concat_axis=0, tiled=True
    ).reshape(capacity, hidden)

    mine = lax.axis_index(GROUP)
    has = jnp.any(routes_all == mine, axis=2)
    rank_all = jnp.dot(has.astype(bf16), before.T, preferred_element_type=f32).astype(jnp.int32)
    pick = (
        has[:, None, :]
        & (rank_all[:, None, :] == jnp.arange(rows, dtype=jnp.int32)[None, :, None])
    ).astype(bf16)
    chosen = (
        lax.dot_general(pick, grads_all, (((2,), (1,)), ((0,), (0,))), preferred_element_type=f32)
        .astype(bf16)
        .reshape(capacity, features)
    )
    grad = lax.dot_general(
        chosen, weight, (((1,), (1,)), ((), ())), preferred_element_type=f32
    ).astype(bf16)
    back = lax.all_to_all(
        grad.reshape(owners, rows, hidden), GROUP, split_axis=0, concat_axis=0, tiled=True
    ).reshape(capacity, hidden)
    part = lax.dot_general(
        recv_act, chosen, (((0,), (0,)), ((), ())), preferred_element_type=f32
    ).astype(bf16)
    weight_grad = lax.psum_scatter(part, "dp", scatter_dimension=0, tiled=True).reshape(
        w_down.shape
    )
    home = jnp.dot(place, back, preferred_element_type=f32)
    act_grad = (home * gate).astype(bf16).reshape(saved_act.shape)
    prob_grad = jnp.sum(home * act.astype(f32), axis=1).reshape(routes.shape)
    return act_grad, prob_grad, weight_grad


def solution(mesh):
    in_specs = (
        P(("dp", "seq", "expert"), None),
        P(("dp", "seq", "expert"), None, None),
        P(("dp", "seq", "expert"), None),
        P(("dp", "seq", "expert"), None),
        P(("seq", "expert"), "dp", None),
    )
    out_specs = (
        P(("dp", "seq", "expert"), None, None),
        P(("dp", "seq", "expert"), None),
        P(("seq", "expert"), "dp", None),
    )
    return jax.shard_map(local, mesh=mesh, in_specs=in_specs, out_specs=out_specs, check_vma=False)
```

time: 500 us -> 229 us (0.46); the launches traced: 491 us -> 229 us
  other arithmetic: 203 us -> 2.15 us
  blocking collectives: 0 us -> 148 us
  local copies, waits for them, and re-layouts: 136 us -> 1.83 us
  waiting for transfers between devices: 86.7 us -> 22.7 us
  starting transfers between devices: 32.8 us -> 7.64 us
  matrix products: 17.9 us -> 32.1 us
    all_to_all x3 -> x0, other arithmetic: 117 us -> none  [the longest x2 77.5 us: local(): lax.all_to_all(back_act, ('seq', 'expert'), split_axis=0, concat_axis=0,...]
    all_gather x0 -> x1, blocking collectives: none -> 100 us  [local(): routes_all = lax.all_gather(routes, GROUP, axis=0)]
    all_to_all x5 -> x1, waiting for transfers between devices: 86 us -> 0.01 us  [local(): lax.all_to_all(packed.reshape(owners, rows, hidden), GROUP, split_axis=0,...]
    convert_element_type x6 -> x0, other arithmetic: 62.8 us -> none  [the longest x1 62.7 us: local(): (recv_prob[:, None] * recv_grad.astype(jnp.float32)).astype(jnp.bfloat16)]
    all_to_all x0 -> x1, blocking collectives: none -> 48.3 us  [local(): lax.all_to_all(grad.reshape(owners, rows, hidden), GROUP, split_axis=0, c...]
    unnamed x19 -> x6, local copies, waits for them, and re-layouts: 41.1 us -> 1.46 us
    gather x7 -> x0, local copies, waits for them, and re-layouts: 29 us -> none  [the longest x2 11.2 us: local(): grad_rows = jnp.take(out_grad, source_row // top_count, axis=0)]
    all_to_all x5 -> x1, starting transfers between devices: 32.7 us -> 7.52 us  [local(): lax.all_to_all(packed.reshape(owners, rows, hidden), GROUP, split_axis=0,...]
  transfers between devices with their start and end apart: 7 -> 4, of which waited for: 3 -> 1; matrix products, arithmetic and copies ran while one was open for 69% -> 16% of each run, Pallas kernels for 0% -> 0%
where the time goes in v1:
time: 229 us
  blocking collectives  148 us (65%)
  matrix products  32.1 us (14%)
  waiting for transfers between devices  22.7 us (10%)
  between operations  13.8 us (6%)
  starting transfers between devices  7.64 us (3%)
    all_gather x1, blocking collectives, local(): routes_all = lax.all_gather(routes, GROUP, axis=0)  100 us
    all_to_all x1, blocking collectives, local(): lax.all_to_all(grad.reshape(owners, rows, hidden), GROUP, split_axis=0, c...  48.3 us
    all_gather x1, waiting for transfers between devices, local(): weight = lax.all_gather(w_down, 'dp', axis=1, tiled=True)[0]  21.3 us
    dot_general x1, matrix products, local(): lax.dot_general(recv_act, chosen, (((0,), (0,)), ((), ())), preferred_ele...  8.01 us
    dot_general x1, matrix products, local(): lax.dot_general(pick, grads_all, (((2,), (1,)), ((0,), (0,))), preferred_...  7.57 us
    all_to_all x1, starting transfers between devices, local(): lax.all_to_all(packed.reshape(owners, rows, hidden), GROUP, split_axis=0,...  7.52 us
    dot_general x1, matrix products, local(): lax.dot_general(chosen, weight, (((1,), (1,)), ((), ())), preferred_eleme...  7.2 us
    dot_general x1, matrix products, local(): lax.dot_general(place, scaled, (((0,), (0,)), ((), ())), preferred_elemen...  5.33 us
  transfers between devices with their start and end apart: 4, of which 1 were waited for; matrix products, arithmetic and copies ran while one was open for 16% of the time, Pallas kernels for 0%

profile of v1, /device:TPU:0, one launch (start us, length us, event | category | flops | bytes accessed | tf_op | source)
XLA Modules:
  0.0 228.7 jit_solution(4062265455509471533)
XLA Ops:
  7.2 0.0 all-gather.7.cloned.1.call-start
  7.2 0.7 all-gather.7.cloned.1.call-update
  7.9 0.7 fusion.17
  8.6 0.1 fusion.16
  8.7 0.7 select_reduce_fusion
  9.5 0.7 convert_add_fusion
  10.2 0.1 copy.15
  10.3 0.1 eq.50
  10.4 0.8 copy.16
  11.1 0.1 mul.31
  11.2 5.3 %fusion.2 = bf16[1152,768]{1,0:T(8,128)(2,1)} fusion(s32[1024]{0:T(1024)S(1)} %eq.50, bf16[128,8,768]{2,1,0:T(8,128)(2,1)} %param.6, f32[1024]{0:T(1024)S(1)} %mul.31), kind=kOutput, calls=%fused_computation.7 | convolution fusion | flops 1816363008 | bytes 3350528 | tf_op jit(solution)/shard_map/dot_general | solution.py:36
  16.6 0.0 copy-start
  16.6 7.5 %all-to-all-start.1 = ((bf16[16,72,768]{2,1,0:T(8,128)(2,1)}), bf16[16,72,768]{2,1,0:T(8,128)(2,1)S(1)}, u32[]{:S(2)}, u32[]{:S(2)}) async-start(bf16[16,72,768]{2,1,0:T(8,128)(2,1)} %bitcast.9), calls=%async_computation.1 | async-start | bytes 3538944 | tf_op jit(solution)/shard_map/all_to_all | solution.py:39
  24.1 0.0 all-gather.5.cloned.1.call-start
  24.1 0.7 all-gather.5.cloned.1.call-update
  24.9 0.0 reduce-scatter.2.cloned.1.call-start
  24.9 0.0 copy-done
  24.9 100.2 %all-gather = s32[2048,8]{0,1:T(8,128)S(1)} all-gather(s32[128,8]{0,1:T(8,128)S(1)} %copy-done), channel_id=2, replica_groups=mesh['dp'=2,'seq'=2,'expert'=8] {'seq','expert'}, dimensions={0}, use_global_device_ids=true | all-gather | bytes 69632 | tf_op jit(solution)/shard_map/all_gather | solution.py:21
  125.2 0.1 convolution_convert_fusion.2
  125.3 0.0 all-gather.7.cloned.1.call-done
  125.3 7.6 %convolution_convert_fusion = bf16[16,72,2048]{2,1,0:T(8,128)(2,1)} fusion(bf16[16,128,2048]{2,1,0:T(8,128)(2,1)} %bitcast.29, s32[16,128]{1,0:T(8,128)S(1)} %convolution_convert_fusion.2, pred[16,128]{1,0:T(8,128)(4,1)S(1)} %bitcast.33), kind=kOutput, calls=%fused_computation.4 | convolution fusion | flops 606633984 | bytes 13117440 | tf_op jit(solution)/shard_map/dot_general | solution.py:51
  132.9 0.0 all-to-all-done.1
  132.9 8.0 %bitcast_convert_fusion = bf16[768,2048]{1,0:T(8,128)(2,1)} fusion(bf16[16,72,768]{2,1,0:T(8,128)(2,1)S(1)} %all-to-all-done.1, bf16[16,72,2048]{2,1,0:T(8,128)(2,1)} %convolution_convert_fusion), kind=kOutput, calls=%fused_computation | convolution fusion | flops 3625451520 | bytes 9633792 | tf_op jit(solution)/shard_map/dot_general | solution.py:61
  140.9 0.0 reduce-scatter.2.cloned.1.call-update
  140.9 21.3 %all-gather.5.cloned.1.call-done = bf16[1,768,2048]{2,1,0:T(8,128)(2,1)} async-done(((bf16[1,384,2048]{2,1,0:T(8,128)(2,1)}), bf16[1,768,2048]{2,1,0:T(8,128)(2,1)}) %all-gather.5.cloned.1.call-update) | async-done | bytes 3145744 | tf_op jit(solution)/shard_map/all_gather | solution.py:22
  162.2 7.2 %convolution_convert_fusion.1 = bf16[1152,768]{1,0:T(8,128)(2,1)S(1)} fusion(bf16[1152,2048]{1,0:T(8,128)(2,1)} %bitcast.30, bf16[1,768,2048]{2,1,0:T(8,128)(2,1)} %all-gather.5.cloned.1.call-done), kind=kOutput, calls=%fused_computation.8 | convolution fusion | flops 3624763392 | bytes 9633792 | tf_op jit(solution)/shard_map/dot_general | solution.py:55
  169.4 0.0 copy-start.1
  169.4 48.3 %all_to_all.10 = bf16[16,72,768]{2,1,0:T(8,128)(2,1)S(1)} all-to-all(bf16[16,72,768]{2,1,0:T(8,128)(2,1)S(1)} %bitcast.32), channel_id=1, replica_groups=mesh['dp'=2,'seq'=2,'expert'=8] {'seq','expert'}, dimensions={0} | all-to-all | bytes 3538944 | tf_op jit(solution)/shard_map/all_to_all | solution.py:58
  217.7 0.0 copy-done.1
  217.7 3.7 %fusion.3 = (f32[1024]{0:T(1024)S(1)}, bf16[128,8,768]{2,1,0:T(8,128)(2,1)}) fusion(bf16[128,8,768]{2,1,0:T(8,128)(2,1)S(1)} %copy-done.1, f32[1024]{0:T(1024)S(1)} %mul.31, bf16[1152,768]{1,0:T(8,128)(2,1)S(1)} %bitcast.31, s32[1024]{0:T(1024)S(1)} %eq.50), kind=kOutput, calls=%fused_computation.9 | convolution fusion | flops 1817050112 | bytes 4927488 | tf_op jit(solution)/shard_map/dot_general | solution.py:67
  221.4 0.1 reshape.42
  221.5 0.7 copy.17
  (2 shorter events, 0.0 us)
Async XLA Ops:
  7.2 118.1 %all-gather.7.cloned.1.call-start = ((), (), s32[]{:S(2)}) async-start(), calls=%async_computation.5 | async-start | bytes 8912896 | tf_op jit(solution)/shard_map/all_gather | solution.py:20
  16.6 8.3 %copy-start = (s32[128,8]{0,1:T(8,128)S(1)}, s32[128,8]{0,1:T(8,128)}, u32[]{:S(2)}) copy-start(s32[128,8]{0,1:T(8,128)} %param.8) | copy-start | bytes 12292
  16.6 116.3 %all-to-all-start.1 = ((bf16[16,72,768]{2,1,0:T(8,128)(2,1)}), bf16[16,72,768]{2,1,0:T(8,128)(2,1)S(1)}, u32[]{:S(2)}, u32[]{:S(2)}) async-start(bf16[16,72,768]{2,1,0:T(8,128)(2,1)} %bitcast.9), calls=%async_computation.1 | async-start | bytes 3538944 | tf_op jit(solution)/shard_map/all_to_all | solution.py:39
  24.1 138.1 %all-gather.5.cloned.1.call-start = ((), (), s32[]{:S(2)}) async-start(), calls=%async_computation.3 | async-start | bytes 4718592 | tf_op jit(solution)/shard_map/all_gather | solution.py:22
  24.9 197.3 %reduce-scatter.2.cloned.1.call-start = ((), (), s32[]{:S(2)}) async-start(), calls=%async_computation.4 | async-start | bytes 4718592 | tf_op jit(solution)/shard_map/reduce_scatter | solution.py:64
  169.4 48.3 %copy-start.1 = (bf16[128,8,768]{2,1,0:T(8,128)(2,1)S(1)}, bf16[128,8,768]{2,1,0:T(8,128)(2,1)}, u32[]{:S(2)}) copy-start(bf16[128,8,768]{2,1,0:T(8,128)(2,1)} %param.6) | copy-start | bytes 4718596
Sparse Core Ops, SparseCore 0:
  10.2 105.7 all-gather.6
  117.6 44.5 all-gather.4
  165.0 43.3 reduce-scatter.1

commit v2 on v1

--- a/solution.py
+++ b/solution.py
@@ -1,9 +1,205 @@
+import functools
+
 import jax
 import jax.numpy as jnp
 from jax import lax
+from jax.experimental import pallas as pl
+from jax.experimental.pallas import tpu as pltpu
 from jax.sharding import PartitionSpec as P
 
 GROUP = ("seq", "expert")
+
+
+def both(*tests):
+    result = tests[0]
+    for test in tests[1:]:
+        result = jnp.logical_and(result, test)
+    return result
+
+
+def gather_kernel(sizes, own, weight, every, weights, here, zs, zr, ys, yr, cs, cr, ws, wr):
+    n_dp, n_seq, n_expert, minor = sizes
+    lines = n_expert // minor
+    dp, seq, expert = lax.axis_index("dp"), lax.axis_index("seq"), lax.axis_index("expert")
+    z, y = expert // minor, expert % minor
+
+    def inside(value, size):
+        return both(value >= 0, value < size)
+
+    peers = [((lax.rem(dp + i, n_dp), seq, expert), None) for i in range(1, n_dp)]
+    peers += [((dp, lax.rem(seq + i, n_seq), expert), None) for i in range(1, n_seq)]
+    for way in (1, -1):
+        peers.append(((dp, seq, expert + way * minor), inside(z + way, lines)))
+        peers.append(((dp, seq, expert + way), inside(y + way, minor)))
+    barrier = pltpu.get_barrier_semaphore()
+
+    def when(test, body):
+        if test is None:
+            body()
+        else:
+            pl.when(test)(body)
+
+    for device, test in peers:
+        when(
+            test,
+            lambda device=device: pl.semaphore_signal(
+                barrier, inc=1, device_id=device, device_id_type=pl.DeviceIdType.MESH
+            ),
+        )
+    count = sum(1 if test is None else test.astype(jnp.int32) for _, test in peers)
+    pl.semaphore_wait(barrier, count)
+
+    sends = []
+
+    def copy(source, target, send, recv, device):
+        return pltpu.make_async_remote_copy(
+            src_ref=source,
+            dst_ref=target,
+            send_sem=send,
+            recv_sem=recv,
+            device_id=device,
+            device_id_type=pl.DeviceIdType.MESH,
+        )
+
+    def start(test, make):
+        when(test, lambda: make().start())
+        sends.append((test, make))
+
+    def place(zb, yb):
+        return seq * n_expert + zb * minor + yb
+
+    def block(zb, yb, is_own):
+        return own if is_own else every.at[place(zb, yb)]
+
+    def z_copy(way, hop):
+        zb = z - way * (hop - 1)
+        return copy(
+            block(zb, y, hop == 1),
+            every.at[place(zb, y)],
+            zs.at[(1 - way) // 2, hop],
+            zr.at[(1 - way) // 2, hop],
+            (dp, seq, expert + way * minor),
+        )
+
+    def y_copy(way, hop, zb, is_own):
+        yb = y - way * (hop - 1)
+        return copy(
+            block(zb, yb, is_own and hop == 1),
+            every.at[place(zb, yb)],
+            ys.at[(1 - way) // 2, hop, zb],
+            yr.at[(1 - way) // 2, hop, zb],
+            (dp, seq, expert + way),
+        )
+
+    def c_copy(i, zb, yb, is_own):
+        return copy(
+            block(zb, yb, is_own),
+            every.at[place(zb, yb)],
+            cs.at[i, zb * minor + yb],
+            cr.at[i, zb * minor + yb],
+            (dp, lax.rem(seq + i, n_seq), expert),
+        )
+
+    def w_copy(i):
+        return copy(
+            weight, weights.at[dp], ws.at[i], wr.at[i], (lax.rem(dp + i, n_dp), seq, expert)
+        )
+
+    def landed(test, ref, sem):
+        when(test, lambda: copy(ref, ref, sem, sem, (dp, seq, expert)).wait_recv())
+
+    def to_cores(test, zb, yb, is_own):
+        for i in range(1, n_seq):
+            start(test, functools.partial(c_copy, i, zb, yb, is_own))
+
+    def spread(test, zb, is_own):
+        for way in (1, -1):
+            go = inside(y + way, minor)
+            go = go if test is None else both(test, go)
+            start(go, functools.partial(y_copy, way, 1, zb, is_own))
+        to_cores(test, zb, y, is_own)
+
+    def arrive_y(test, zb):
+        for hop in range(1, minor):
+            for way in (1, -1):
+                yb = y - way * hop
+                got = inside(yb, minor)
+                got = got if test is None else both(test, got)
+                landed(got, every.at[place(zb, yb)], yr.at[(1 - way) // 2, hop, zb])
+                if hop + 1 < minor:
+                    start(
+                        both(got, inside(y + way, minor)),
+                        functools.partial(y_copy, way, hop + 1, zb, False),
+                    )
+                to_cores(got, zb, yb, False)
+
+    for way in (1, -1):
+        start(inside(z + way, lines), functools.partial(z_copy, way, 1))
+    spread(None, z, True)
+    for i in range(1, n_dp):
+        start(None, functools.partial(w_copy, i))
+    locals_ = [
+        pltpu.make_async_copy(own, every.at[place(z, y)], here.at[0]),
+        pltpu.make_async_copy(weight, weights.at[dp], here.at[1]),
+    ]
+    for one in locals_:
+        one.start()
+    waiting = [(None, z)]
+    for hop in range(1, lines):
+        fresh = []
+        for way in (1, -1):
+            zb = z - way * hop
+            got = inside(zb, lines)
+            landed(got, every.at[place(zb, y)], zr.at[(1 - way) // 2, hop])
+            if hop + 1 < lines:
+                start(both(got, inside(z + way, lines)), functools.partial(z_copy, way, hop + 1))
+            spread(got, zb, False)
+            fresh.append((got, zb))
+        for test, zb in waiting:
+            arrive_y(test, zb)
+        waiting = fresh
+    for test, zb in waiting:
+        arrive_y(test, zb)
+    for i in range(1, n_seq):
+        other = lax.rem(seq - i + n_seq, n_seq)
+        for e in range(n_expert):
+            landed(None, every.at[other * n_expert + e], cr.at[i, e])
+    for i in range(1, n_dp):
+        landed(None, weights.at[lax.rem(dp - i + n_dp, n_dp)], wr.at[i])
+    for test, make in sends:
+        when(test, lambda make=make: make().wait_send())
+    for one in locals_:
+        one.wait()
+
+
+def gather(out_grad, weight):
+    n_dp, n_seq, n_expert = (lax.axis_size(name) for name in ("dp", "seq", "expert"))
+    minor = 1 << ((n_expert.bit_length() - 1) // 2)
+    lines = n_expert // minor
+    sems = pltpu.SemaphoreType.DMA
+    hbm = pl.BlockSpec(memory_space=pl.ANY)
+    return pl.pallas_call(
+        functools.partial(gather_kernel, (n_dp, n_seq, n_expert, minor)),
+        out_shape=(
+            jax.ShapeDtypeStruct((n_seq * n_expert,) + out_grad.shape, out_grad.dtype),
+            jax.ShapeDtypeStruct((n_dp,) + weight.shape, weight.dtype),
+        ),
+        in_specs=[hbm, hbm],
+        out_specs=(hbm, hbm),
+        scratch_shapes=[
+            sems((2,)),
+            sems((2, lines)),
+            sems((2, lines)),
+            sems((2, minor, lines)),
+            sems((2, minor, lines)),
+            sems((n_seq, n_expert)),
+            sems((n_seq, n_expert)),
+            sems((n_dp,)),
+            sems((n_dp,)),
+        ],
+        compiler_params=pltpu.CompilerParams(collective_id=0, has_side_effects=True),
+        name="gather",
+    )(out_grad, weight)
 
 
 def local(out_grad, saved_act, gate_probs, routes, w_down):
@@ -17,9 +213,9 @@
     capacity = owners * rows
     f32, bf16 = jnp.float32, jnp.bfloat16
 
-    grads_all = lax.all_gather(out_grad, GROUP, axis=0)
+    grads_all, weight = gather(out_grad, w_down[0])
+    weight = weight.reshape(-1, features)
     routes_all = lax.all_gather(routes, GROUP, axis=0)
-    weight = lax.all_gather(w_down, "dp", axis=1, tiled=True)[0]
 
     ids = jnp.arange(owners, dtype=jnp.int32)
     named = routes[:, :, None] == ids[None, None, :]

time: 229 us -> 229 us (level)
  Pallas kernels: 0 us -> 95 us
  blocking collectives: 148 us -> 75.7 us
  waiting for transfers between devices: 22.7 us -> 0.02 us
    pallas_call x0 -> x1, Pallas kernels: none -> 95 us  [gather(): pl.pallas_call(functools.partial(gather_kernel, (n_dp, n_seq, n_expert, m...]
    all_gather x1, blocking collectives: 100 us -> 29.4 us  [local(): routes_all = lax.all_gather(routes, GROUP, axis=0)]
    all_gather x2 -> x0, waiting for transfers between devices: 21.3 us -> none  [the longest x1 21.3 us: local(): weight = lax.all_gather(w_down, 'dp', axis=1, tiled=True)[0]]
  transfers between devices with their start and end apart: 4 -> 2, of which waited for: 1 -> 0; matrix products, arithmetic and copies ran while one was open for 16% -> 8% of each run, Pallas kernels for 0% -> 42%
where the time goes in v2:
time: 229 us
  Pallas kernels  95 us (41%)
  blocking collectives  75.7 us (33%)
  matrix products  30.5 us (13%)
  between operations  14.1 us (6%)
  starting transfers between devices  7.56 us (3%)
  local copies, waits for them, and re-layouts  3.69 us (2%)
    pallas_call x1, Pallas kernels, gather(): pl.pallas_call(functools.partial(gather_kernel, (n_dp, n_seq, n_expert, m...  95 us
    all_to_all x1, blocking collectives, local(): lax.all_to_all(grad.reshape(owners, rows, hidden), GROUP, split_axis=0, c...  46.3 us
    all_gather x1, blocking collectives, local(): routes_all = lax.all_gather(routes, GROUP, axis=0)  29.4 us
    dot_general x1, matrix products, local(): lax.dot_general(recv_act, chosen, (((0,), (0,)), ((), ())), preferred_ele...  8.01 us
    all_to_all x1, starting transfers between devices, local(): lax.all_to_all(packed.reshape(owners, rows, hidden), GROUP, split_axis=0,...  7.52 us
    dot_general x1, matrix products, local(): lax.dot_general(pick, grads_all, (((2,), (1,)), ((0,), (0,))), preferred_...  6.92 us
    dot_general x1, matrix products, local(): lax.dot_general(chosen, weight, (((1,), (1,)), ((), ())), preferred_eleme...  6.22 us
    dot_general x1, matrix products, local(): lax.dot_general(place, scaled, (((0,), (0,)), ((), ())), preferred_elemen...  5.33 us
  transfers between devices with their start and end apart: 2, of which 0 were waited for; matrix products, arithmetic and copies ran while one was open for 8% of the time, Pallas kernels for 42%

profile of v2, /device:TPU:0, one launch (start us, length us, event | category | flops | bytes accessed | tf_op | source)
XLA Modules:
  0.0 228.7 jit_solution(13236083980468725554)
XLA Ops:
  7.2 0.7 fusion.16
  7.9 0.1 fusion.15
  8.0 0.7 select_reduce_fusion
  8.7 0.7 convert_add_fusion
  9.4 0.1 copy.15
  9.5 0.1 eq.50
  9.6 0.8 copy.16
  10.4 0.1 mul.31
  10.5 5.3 %fusion.2 = bf16[1152,768]{1,0:T(8,128)(2,1)} fusion(s32[1024]{0:T(1024)S(1)} %eq.50, bf16[128,8,768]{2,1,0:T(8,128)(2,1)} %param.6, f32[1024]{0:T(1024)S(1)} %mul.31), kind=kOutput, calls=%fused_computation.7 | convolution fusion | flops 1816363008 | bytes 3350528 | tf_op jit(solution)/shard_map/dot_general | solution.py:232
  15.8 0.0 copy-start
  15.8 7.5 %all-to-all-start.1 = ((bf16[16,72,768]{2,1,0:T(8,128)(2,1)}), bf16[16,72,768]{2,1,0:T(8,128)(2,1)S(1)}, u32[]{:S(2)}, u32[]{:S(2)}) async-start(bf16[16,72,768]{2,1,0:T(8,128)(2,1)} %bitcast.9), calls=%async_computation.1 | async-start | bytes 3538944 | tf_op jit(solution)/shard_map/all_to_all | solution.py:235
  23.4 0.0 reduce-scatter.2.cloned.1.call-start
  23.4 95.0 %gather.1 = (bf16[16,128,2048]{2,1,0:T(8,128)(2,1)}, bf16[2,384,2048]{2,1,0:T(8,128)(2,1)}) custom-call(bf16[128,2048]{1,0:T(8,128)(2,1)} %own.1, bf16[384,2048]{1,0:T(8,128)(2,1)} %bitcast.31), custom_call_target="tpu_custom_call" | custom-call | tf_op jit(solution)/shard_map/gather/pallas_call | solution.py:181
  118.4 0.0 copy-done
  118.5 29.4 %all-gather = s32[2048,8]{0,1:T(8,128)S(1)} all-gather(s32[128,8]{0,1:T(8,128)S(1)} %copy-done), channel_id=2, replica_groups=mesh['dp'=2,'seq'=2,'expert'=8] {'seq','expert'}, dimensions={0}, use_global_device_ids=true | all-gather | bytes 69632 | tf_op jit(solution)/shard_map/all_gather | solution.py:218
  147.9 0.1 convolution_convert_fusion.2
  148.0 6.9 %convolution_convert_fusion = bf16[16,72,2048]{2,1,0:T(8,128)(2,1)} fusion(bf16[16,128,2048]{2,1,0:T(8,128)(2,1)} %get-tuple-element.5, s32[16,128]{1,0:T(8,128)S(1)} %convolution_convert_fusion.2, pred[16,128]{1,0:T(8,128)(4,1)S(1)} %bitcast.32), kind=kOutput, calls=%fused_computation.4 | convolution fusion | flops 606633984 | bytes 13117440 | tf_op jit(solution)/shard_map/dot_general | solution.py:247
  154.9 0.0 all-to-all-done.1
  154.9 8.0 %bitcast_convert_fusion = bf16[768,2048]{1,0:T(8,128)(2,1)} fusion(bf16[16,72,768]{2,1,0:T(8,128)(2,1)S(1)} %all-to-all-done.1, bf16[16,72,2048]{2,1,0:T(8,128)(2,1)} %convolution_convert_fusion), kind=kOutput, calls=%fused_computation | convolution fusion | flops 3625451520 | bytes 9633792 | tf_op jit(solution)/shard_map/dot_general | solution.py:257
  163.0 0.0 copy-start.1
  163.0 0.0 reduce-scatter.2.cloned.1.call-update
  163.0 1.9 copy-done.1
  164.8 6.2 %convolution_convert_fusion.1 = bf16[1152,768]{1,0:T(8,128)(2,1)S(1)} fusion(bf16[1152,2048]{1,0:T(8,128)(2,1)} %bitcast.28, bf16[768,2048]{1,0:T(8,128)(2,1)S(1)} %bitcast.33), kind=kOutput, calls=%fused_computation.8 | convolution fusion | flops 3624763392 | bytes 9633792 | tf_op jit(solution)/shard_map/dot_general | solution.py:251
  171.1 0.0 copy-start.2
  171.1 46.3 %all_to_all.10 = bf16[16,72,768]{2,1,0:T(8,128)(2,1)S(1)} all-to-all(bf16[16,72,768]{2,1,0:T(8,128)(2,1)S(1)} %bitcast.30), channel_id=1, replica_groups=mesh['dp'=2,'seq'=2,'expert'=8] {'seq','expert'}, dimensions={0} | all-to-all | bytes 3538944 | tf_op jit(solution)/shard_map/all_to_all | solution.py:254
  217.4 0.0 copy-done.2
  217.4 3.7 %fusion.3 = (f32[1024]{0:T(1024)S(1)}, bf16[128,8,768]{2,1,0:T(8,128)(2,1)}) fusion(bf16[128,8,768]{2,1,0:T(8,128)(2,1)S(1)} %copy-done.2, f32[1024]{0:T(1024)S(1)} %mul.31, bf16[1152,768]{1,0:T(8,128)(2,1)S(1)} %bitcast.29, s32[1024]{0:T(1024)S(1)} %eq.50), kind=kOutput, calls=%fused_computation.9 | convolution fusion | flops 1817050112 | bytes 4927488 | tf_op jit(solution)/shard_map/dot_general | solution.py:263
  221.1 0.1 reshape.46
  221.2 0.7 copy.17
  221.8 0.0 reduce-scatter.2.cloned.1.call-done
  (1 shorter events, 0.0 us)
Async XLA Ops:
  15.8 102.6 %copy-start = (s32[128,8]{0,1:T(8,128)S(1)}, s32[128,8]{0,1:T(8,128)}, u32[]{:S(2)}) copy-start(s32[128,8]{0,1:T(8,128)} %param.8) | copy-start | bytes 12292
  15.8 139.1 %all-to-all-start.1 = ((bf16[16,72,768]{2,1,0:T(8,128)(2,1)}), bf16[16,72,768]{2,1,0:T(8,128)(2,1)S(1)}, u32[]{:S(2)}, u32[]{:S(2)}) async-start(bf16[16,72,768]{2,1,0:T(8,128)(2,1)} %bitcast.9), calls=%async_computation.1 | async-start | bytes 3538944 | tf_op jit(solution)/shard_map/all_to_all | solution.py:235
  23.4 198.5 %reduce-scatter.2.cloned.1.call-start = ((), (), s32[]{:S(2)}) async-start(), calls=%async_computation.3 | async-start | bytes 4718592 | tf_op jit(solution)/shard_map/reduce_scatter | solution.py:260
  163.0 1.9 copy-start.1
  171.1 46.3 %copy-start.2 = (bf16[128,8,768]{2,1,0:T(8,128)(2,1)S(1)}, bf16[128,8,768]{2,1,0:T(8,128)(2,1)}, u32[]{:S(2)}) copy-start(bf16[128,8,768]{2,1,0:T(8,128)(2,1)} %param.6) | copy-start | bytes 4718596
Sparse Core Ops, SparseCore 0:
  163.1 42.2 reduce-scatter.1

commit v3 on v2

--- a/solution.py
+++ b/solution.py
@@ -17,7 +17,9 @@
     return result
 
 
-def gather_kernel(sizes, own, weight, every, weights, here, zs, zr, ys, yr, cs, cr, ws, wr):
+def gather_kernel(
+    sizes, own, weight, named, every, weights, names, here, zs, zr, ys, yr, cs, cr, ws, wr, rs, rr
+):
     n_dp, n_seq, n_expert, minor = sizes
     lines = n_expert // minor
     dp, seq, expert = lax.axis_index("dp"), lax.axis_index("seq"), lax.axis_index("expert")
@@ -26,28 +28,29 @@
     def inside(value, size):
         return both(value >= 0, value < size)
 
-    peers = [((lax.rem(dp + i, n_dp), seq, expert), None) for i in range(1, n_dp)]
-    peers += [((dp, lax.rem(seq + i, n_seq), expert), None) for i in range(1, n_seq)]
-    for way in (1, -1):
-        peers.append(((dp, seq, expert + way * minor), inside(z + way, lines)))
-        peers.append(((dp, seq, expert + way), inside(y + way, minor)))
+    n_group = n_seq * n_expert
+    me = seq * n_expert + expert
     barrier = pltpu.get_barrier_semaphore()
+
+    def member(i):
+        index = lax.rem(me + i, n_group)
+        return (dp, index // n_expert, lax.rem(index, n_expert))
+
+    def greet(device):
+        pl.semaphore_signal(
+            barrier, inc=1, device_id=device, device_id_type=pl.DeviceIdType.MESH
+        )
+
+    lax.fori_loop(1, n_group, lambda i, _: greet(member(i)), None)
+    for i in range(1, n_dp):
+        greet((lax.rem(dp + i, n_dp), seq, expert))
+    pl.semaphore_wait(barrier, n_group + n_dp - 2)
 
     def when(test, body):
         if test is None:
             body()
         else:
             pl.when(test)(body)
-
-    for device, test in peers:
-        when(
-            test,
-            lambda device=device: pl.semaphore_signal(
-                barrier, inc=1, device_id=device, device_id_type=pl.DeviceIdType.MESH
-            ),
-        )
-    count = sum(1 if test is None else test.astype(jnp.int32) for _, test in peers)
-    pl.semaphore_wait(barrier, count)
 
     sends = []
 
@@ -133,12 +136,17 @@
                     )
                 to_cores(got, zb, yb, False)
 
+    def r_copy(i):
+        return copy(named, names.at[me], rs.at[i], rr.at[i], member(i))
+
     for way in (1, -1):
         start(inside(z + way, lines), functools.partial(z_copy, way, 1))
     spread(None, z, True)
     for i in range(1, n_dp):
         start(None, functools.partial(w_copy, i))
+    lax.fori_loop(1, n_group, lambda i, _: r_copy(i).start(), None)
     locals_ = [
+        pltpu.make_async_copy(named, names.at[me], here.at[2]),
         pltpu.make_async_copy(own, every.at[place(z, y)], here.at[0]),
         pltpu.make_async_copy(weight, weights.at[dp], here.at[1]),
     ]
@@ -166,13 +174,19 @@
             landed(None, every.at[other * n_expert + e], cr.at[i, e])
     for i in range(1, n_dp):
         landed(None, weights.at[lax.rem(dp - i + n_dp, n_dp)], wr.at[i])
+
+    def finish(i, _):
+        landed(None, names.at[lax.rem(me - i + n_group, n_group)], rr.at[i])
+        r_copy(i).wait_send()
+
+    lax.fori_loop(1, n_group, finish, None)
     for test, make in sends:
         when(test, lambda make=make: make().wait_send())
     for one in locals_:
         one.wait()
 
 
-def gather(out_grad, weight):
+def gather(out_grad, weight, named):
     n_dp, n_seq, n_expert = (lax.axis_size(name) for name in ("dp", "seq", "expert"))
     minor = 1 << ((n_expert.bit_length() - 1) // 2)
     lines = n_expert // minor
@@ -183,11 +197,12 @@
         out_shape=(
             jax.ShapeDtypeStruct((n_seq * n_expert,) + out_grad.shape, out_grad.dtype),
             jax.ShapeDtypeStruct((n_dp,) + weight.shape, weight.dtype),
+            jax.ShapeDtypeStruct((n_seq * n_expert,) + named.shape, named.dtype),
         ),
-        in_specs=[hbm, hbm],
-        out_specs=(hbm, hbm),
+        in_specs=[hbm, hbm, hbm],
+        out_specs=(hbm, hbm, hbm),
         scratch_shapes=[
-            sems((2,)),
+            sems((3,)),
             sems((2, lines)),
             sems((2, lines)),
             sems((2, minor, lines)),
@@ -196,10 +211,12 @@
             sems((n_seq, n_expert)),
             sems((n_dp,)),
             sems((n_dp,)),
+            sems((n_seq * n_expert,)),
+            sems((n_seq * n_expert,)),
         ],
         compiler_params=pltpu.CompilerParams(collective_id=0, has_side_effects=True),
         name="gather",
-    )(out_grad, weight)
+    )(out_grad, weight, named)
 
 
 def local(out_grad, saved_act, gate_probs, routes, w_down):
@@ -213,9 +230,8 @@
     capacity = owners * rows
     f32, bf16 = jnp.float32, jnp.bfloat16
 
-    grads_all, weight = gather(out_grad, w_down[0])
+    grads_all, weight, routes_all = gather(out_grad, w_down[0], routes.T)
     weight = weight.reshape(-1, features)
-    routes_all = lax.all_gather(routes, GROUP, axis=0)
 
     ids = jnp.arange(owners, dtype=jnp.int32)
     named = routes[:, :, None] == ids[None, None, :]
@@ -232,12 +248,13 @@
     packed = lax.dot_general(
         place, scaled, (((0,), (0,)), ((), ())), preferred_element_type=f32
     ).astype(bf16)
+    packed, grads_all, routes_all = lax.optimization_barrier((packed, grads_all, routes_all))
     recv_act = lax.all_to_all(
         packed.reshape(owners, rows, hidden), GROUP, split_axis=0, concat_axis=0, tiled=True
     ).reshape(capacity, hidden)
 
     mine = lax.axis_index(GROUP)
-    has = jnp.any(routes_all == mine, axis=2)
+    has = jnp.any(routes_all == mine, axis=1)
     rank_all = jnp.dot(has.astype(bf16), before.T, preferred_element_type=f32).astype(jnp.int32)
     pick = (
         has[:, None, :]
@@ -254,6 +271,7 @@
     back = lax.all_to_all(
         grad.reshape(owners, rows, hidden), GROUP, split_axis=0, concat_axis=0, tiled=True
     ).reshape(capacity, hidden)
+    recv_act, _ = lax.optimization_barrier((recv_act, grad))
     part = lax.dot_general(
         recv_act, chosen, (((0,), (0,)), ((), ())), preferred_element_type=f32
     ).astype(bf16)

time: 229 us -> 200 us (0.87)
  waiting for transfers between devices: 0.02 us -> 29.6 us
  blocking collectives: 75.7 us -> 47.3 us
  Pallas kernels: 95 us -> 72.4 us
  matrix products: 30.5 us -> 26.3 us
  starting transfers between devices: 7.56 us -> 3.9 us
    all_to_all x1, waiting for transfers between devices: 0.01 us -> 29.6 us  [local(): lax.all_to_all(packed.reshape(owners, rows, hidden), GROUP, split_axis=0,...]
    all_gather x1 -> x0, blocking collectives: 29.4 us -> none  [local(): routes_all = lax.all_gather(routes, GROUP, axis=0)]
    pallas_call x1, Pallas kernels: 95 us -> 72.4 us  [gather(): pl.pallas_call(functools.partial(gather_kernel, (n_dp, n_seq, n_expert, m...]
    all_to_all x1, starting transfers between devices: 7.52 us -> 3.85 us  [local(): lax.all_to_all(packed.reshape(owners, rows, hidden), GROUP, split_axis=0,...]
  transfers between devices with their start and end apart: 2 -> 2, of which waited for: 0 -> 1; matrix products, arithmetic and copies ran while one was open for 8% -> 7% of each run, Pallas kernels for 42% -> 0%
where the time goes in v3:
time: 200 us
  Pallas kernels  72.4 us (36%)
  blocking collectives  47.3 us (24%)
  waiting for transfers between devices  29.6 us (15%)
  matrix products  26.3 us (13%)
  between operations  14.1 us (7%)
  local copies, waits for them, and re-layouts  3.95 us (2%)
  starting transfers between devices  3.9 us (2%)
  other arithmetic  2.16 us (1%)
    pallas_call x1, Pallas kernels, gather(): pl.pallas_call(functools.partial(gather_kernel, (n_dp, n_seq, n_expert, m...  72.4 us
    all_to_all x1, blocking collectives, local(): lax.all_to_all(grad.reshape(owners, rows, hidden), GROUP, split_axis=0, c...  47.3 us
    all_to_all x1, waiting for transfers between devices, local(): lax.all_to_all(packed.reshape(owners, rows, hidden), GROUP, split_axis=0,...  29.6 us
    dot_general x1, matrix products, local(): lax.dot_general(recv_act, chosen, (((0,), (0,)), ((), ())), preferred_ele...  7.98 us
    dot_general x1, matrix products, local(): lax.dot_general(place, scaled, (((0,), (0,)), ((), ())), preferred_elemen...  5.4 us
    dot_general x1, matrix products, local(): lax.dot_general(pick, grads_all, (((2,), (1,)), ((0,), (0,))), preferred_...  4.92 us
  transfers between devices with their start and end apart: 2, of which 1 were waited for; matrix products, arithmetic and copies ran while one was open for 7% of the time, Pallas kernels for 0%

profile of v3, /device:TPU:0, one launch (start us, length us, event | category | flops | bytes accessed | tf_op | source)
XLA Modules:
  0.0 199.7 jit_solution(10801390362989214752)
XLA Ops:
  7.2 0.7 fusion.16
  7.9 0.1 fusion.15
  8.0 0.7 select_reduce_fusion
  8.7 0.7 convert_add_fusion
  9.4 0.1 copy.15
  9.5 0.1 eq.50
  9.6 0.8 copy.16
  10.4 0.1 mul.30
  10.5 5.4 %fusion.2 = bf16[1152,768]{1,0:T(8,128)(2,1)} fusion(s32[1024]{0:T(1024)S(1)} %eq.50, bf16[128,8,768]{2,1,0:T(8,128)(2,1)} %param.6, f32[1024]{0:T(1024)S(1)} %mul.30), kind=kOutput, calls=%fused_computation.6 | convolution fusion | flops 1816363008 | bytes 3350528 | tf_op jit(solution)/shard_map/dot_general | solution.py:248
  15.9 72.4 %gather.1 = (bf16[16,128,2048]{2,1,0:T(8,128)(2,1)}, bf16[2,384,2048]{2,1,0:T(8,128)(2,1)}, s32[16,8,128]{2,1,0:T(8,128)}) custom-call(bf16[128,2048]{1,0:T(8,128)(2,1)} %own.1, bf16[384,2048]{1,0:T(8,128)(2,1)} %bitcast.31, s32[8,128]{1,0:T(8,128)} %bitcast.32), custom_call_target="tpu_custom_call" | custom-call | tf_op jit(solution)/shard_map/gather/pallas_call | solution.py:195
  88.3 0.0 copy-start.1
  88.3 3.9 %all-to-all-start.1 = ((bf16[16,72,768]{2,1,0:T(8,128)(2,1)}), bf16[16,72,768]{2,1,0:T(8,128)(2,1)S(1)}, u32[]{:S(2)}, u32[]{:S(2)}) async-start(bf16[16,72,768]{2,1,0:T(8,128)(2,1)} %bitcast.9), calls=%async_computation.1 | async-start | bytes 3538944 | tf_op jit(solution)/shard_map/all_to_all | solution.py:252
  92.1 0.0 reduce-scatter.2.cloned.1.call-start
  92.2 0.0 copy-done.1
  92.2 0.1 convolution_convert_fusion.3
  92.4 0.0 copy-start.2
  92.4 4.9 %convolution_convert_fusion = bf16[16,72,2048]{2,1,0:T(8,128)(2,1)S(1)} fusion(bf16[16,128,2048]{2,1,0:T(8,128)(2,1)} %get-tuple-element.13, s32[16,128]{1,0:T(8,128)S(1)} %convolution_convert_fusion.3, pred[16,128]{1,0:T(8,128)(4,1)S(1)} %compare_reduce_fusion), kind=kOutput, calls=%fused_computation.3 | convolution fusion | flops 606633984 | bytes 13117440 | tf_op jit(solution)/shard_map/dot_general | solution.py:264
  97.3 0.0 copy-start
  97.3 2.1 %copy-done = bf16[16,72,2048]{2,1,0:T(8,128)(2,1)} copy-done((bf16[16,72,2048]{2,1,0:T(8,128)(2,1)}, bf16[16,72,2048]{2,1,0:T(8,128)(2,1)S(1)}, u32[]{:S(2)}) %copy-start) | copy-done | bytes 4718616
  99.4 0.0 copy-done.2
  99.4 4.0 %convolution_convert_fusion.2 = bf16[1152,768]{1,0:T(8,128)(2,1)S(1)} fusion(bf16[1152,2048]{1,0:T(8,128)(2,1)S(1)} %bitcast.26, bf16[768,2048]{1,0:T(8,128)(2,1)S(1)} %bitcast.33), kind=kOutput, calls=%fused_computation.8 | convolution fusion | flops 3624763392 | bytes 9633792 | tf_op jit(solution)/shard_map/dot_general | solution.py:268
  103.4 29.6 %all-to-all-done.1 = bf16[16,72,768]{2,1,0:T(8,128)(2,1)S(1)} async-done(((bf16[16,72,768]{2,1,0:T(8,128)(2,1)}), bf16[16,72,768]{2,1,0:T(8,128)(2,1)S(1)}, u32[]{:S(2)}, u32[]{:S(2)}) %all-to-all-start.1) | async-done | bytes 1769504 | tf_op jit(solution)/shard_map/all_to_all | solution.py:252
  133.0 8.0 %convolution_convert_fusion.1 = bf16[768,2048]{1,0:T(8,128)(2,1)} fusion(bf16[1152,768]{1,0:T(8,128)(2,1)S(1)} %bitcast.28, bf16[1152,2048]{1,0:T(8,128)(2,1)} %bitcast.27), kind=kOutput, calls=%fused_computation.7 | convolution fusion | flops 3625451520 | bytes 9633792 | tf_op jit(solution)/shard_map/dot_general | solution.py:275
  141.0 0.0 copy-start.3
  141.0 0.0 reduce-scatter.2.cloned.1.call-update
  141.0 47.3 %all_to_all.10 = bf16[16,72,768]{2,1,0:T(8,128)(2,1)S(1)} all-to-all(bf16[16,72,768]{2,1,0:T(8,128)(2,1)S(1)} %bitcast.29), channel_id=1, replica_groups=mesh['dp'=2,'seq'=2,'expert'=8] {'seq','expert'}, dimensions={0} | all-to-all | bytes 3538944 | tf_op jit(solution)/shard_map/all_to_all | solution.py:271
  188.3 0.0 copy-done.3
  188.3 3.8 %fusion.4 = (f32[1024]{0:T(1024)S(1)}, bf16[128,8,768]{2,1,0:T(8,128)(2,1)}) fusion(bf16[128,8,768]{2,1,0:T(8,128)(2,1)S(1)} %copy-done.3, f32[1024]{0:T(1024)S(1)} %mul.30, bf16[1152,768]{1,0:T(8,128)(2,1)S(1)} %bitcast.30, s32[1024]{0:T(1024)S(1)} %eq.50), kind=kOutput, calls=%fused_computation.10 | convolution fusion | flops 1817050112 | bytes 4927488 | tf_op jit(solution)/shard_map/dot_general | solution.py:281
  192.1 0.1 reshape.48
  192.2 0.7 copy.17
  192.8 0.0 reduce-scatter.2.cloned.1.call-done
  (1 shorter events, 0.0 us)
Async XLA Ops:
  88.3 3.9 %copy-start.1 = (s32[16,8,128]{2,1,0:T(8,128)S(1)}, s32[16,8,128]{2,1,0:T(8,128)}, u32[]{:S(2)}) copy-start(s32[16,8,128]{2,1,0:T(8,128)} %get-tuple-element.12) | copy-start | bytes 196612
  88.3 44.8 %all-to-all-start.1 = ((bf16[16,72,768]{2,1,0:T(8,128)(2,1)}), bf16[16,72,768]{2,1,0:T(8,128)(2,1)S(1)}, u32[]{:S(2)}, u32[]{:S(2)}) async-start(bf16[16,72,768]{2,1,0:T(8,128)(2,1)} %bitcast.9), calls=%async_computation.1 | async-start | bytes 3538944 | tf_op jit(solution)/shard_map/all_to_all | solution.py:252
  92.1 100.7 %reduce-scatter.2.cloned.1.call-start = ((), (), s32[]{:S(2)}) async-start(), calls=%async_computation.3 | async-start | bytes 4718592 | tf_op jit(solution)/shard_map/reduce_scatter | solution.py:278
  92.4 7.1 %copy-start.2 = (bf16[2,384,2048]{2,1,0:T(8,128)(2,1)S(1)}, bf16[2,384,2048]{2,1,0:T(8,128)(2,1)}, u32[]{:S(2)}) copy-start(bf16[2,384,2048]{2,1,0:T(8,128)(2,1)} %get-tuple-element.14) | copy-start | bytes 9437188
  97.3 2.1 %copy-start = (bf16[16,72,2048]{2,1,0:T(8,128)(2,1)}, bf16[16,72,2048]{2,1,0:T(8,128)(2,1)S(1)}, u32[]{:S(2)}) copy-start(bf16[16,72,2048]{2,1,0:T(8,128)(2,1)S(1)} %convolution_convert_fusion) | copy-start | bytes 14155780
  141.0 47.3 %copy-start.3 = (bf16[128,8,768]{2,1,0:T(8,128)(2,1)S(1)}, bf16[128,8,768]{2,1,0:T(8,128)(2,1)}, u32[]{:S(2)}) copy-start(bf16[128,8,768]{2,1,0:T(8,128)(2,1)} %param.6) | copy-start | bytes 4718596
Sparse Core Ops, SparseCore 0:
  141.2 43.2 reduce-scatter.1

commit v4 on v3

--- a/solution.py
+++ b/solution.py
@@ -18,7 +18,8 @@
 
 
 def gather_kernel(
-    sizes, own, weight, named, every, weights, names, here, zs, zr, ys, yr, cs, cr, ws, wr, rs, rr
+    sizes, own, weight, named, packed, every, weights, names, acts,
+    here, zs, zr, ys, yr, cs, cr, ws, wr, rs, rr, sa, ra
 ):
     n_dp, n_seq, n_expert, minor = sizes
     lines = n_expert // minor
@@ -139,6 +140,10 @@
     def r_copy(i):
         return copy(named, names.at[me], rs.at[i], rr.at[i], member(i))
 
+    def a_copy(i):
+        index = lax.rem(me + i, n_group)
+        return copy(packed.at[index], acts.at[me], sa.at[i], ra.at[i], member(i))
+
     for way in (1, -1):
         start(inside(z + way, lines), functools.partial(z_copy, way, 1))
     spread(None, z, True)
@@ -147,6 +152,7 @@
     lax.fori_loop(1, n_group, lambda i, _: r_copy(i).start(), None)
     locals_ = [
         pltpu.make_async_copy(named, names.at[me], here.at[2]),
+        pltpu.make_async_copy(packed.at[me], acts.at[me], here.at[3]),
         pltpu.make_async_copy(own, every.at[place(z, y)], here.at[0]),
         pltpu.make_async_copy(weight, weights.at[dp], here.at[1]),
     ]
@@ -166,6 +172,7 @@
         for test, zb in waiting:
             arrive_y(test, zb)
         waiting = fresh
+    lax.fori_loop(1, n_group, lambda i, _: a_copy(i).start(), None)
     for test, zb in waiting:
         arrive_y(test, zb)
     for i in range(1, n_seq):
@@ -178,6 +185,8 @@
     def finish(i, _):
         landed(None, names.at[lax.rem(me - i + n_group, n_group)], rr.at[i])
         r_copy(i).wait_send()
+        landed(None, acts.at[lax.rem(me - i + n_group, n_group)], ra.at[i])
+        a_copy(i).wait_send()
 
     lax.fori_loop(1, n_group, finish, None)
     for test, make in sends:
@@ -186,7 +195,7 @@
         one.wait()
 
 
-def gather(out_grad, weight, named):
+def gather(out_grad, weight, named, packed):
     n_dp, n_seq, n_expert = (lax.axis_size(name) for name in ("dp", "seq", "expert"))
     minor = 1 << ((n_expert.bit_length() - 1) // 2)
     lines = n_expert // minor
@@ -198,11 +207,12 @@
             jax.ShapeDtypeStruct((n_seq * n_expert,) + out_grad.shape, out_grad.dtype),
             jax.ShapeDtypeStruct((n_dp,) + weight.shape, weight.dtype),
             jax.ShapeDtypeStruct((n_seq * n_expert,) + named.shape, named.dtype),
+            jax.ShapeDtypeStruct(packed.shape, packed.dtype),
         ),
-        in_specs=[hbm, hbm, hbm],
-        out_specs=(hbm, hbm, hbm),
+        in_specs=[hbm] * 4,
+        out_specs=(hbm,) * 4,
         scratch_shapes=[
-            sems((3,)),
+            sems((4,)),
             sems((2, lines)),
             sems((2, lines)),
             sems((2, minor, lines)),
@@ -213,10 +223,12 @@
             sems((n_dp,)),
             sems((n_seq * n_expert,)),
             sems((n_seq * n_expert,)),
+            sems((n_seq * n_expert,)),
+            sems((n_seq * n_expert,)),
         ],
         compiler_params=pltpu.CompilerParams(collective_id=0, has_side_effects=True),
         name="gather",
-    )(out_grad, weight, named)
+    )(out_grad, weight, named, packed)
 
 
 def local(out_grad, saved_act, gate_probs, routes, w_down):
@@ -227,11 +239,13 @@
     pairs = tokens * top
     most = max(2, min(tokens, pairs // owners + pairs // (8 * owners)))
     rows = -(-most // 8) * 8
+    tall = rows * 2 // 3
+    folds = rows % 16 != 0 and rows % 24 == 0 and tall % 16 == 0 and hidden % 256 == 0
+    if not folds:
+        rows = -(-rows // 16) * 16
     capacity = owners * rows
     f32, bf16 = jnp.float32, jnp.bfloat16
 
-    grads_all, weight, routes_all = gather(out_grad, w_down[0], routes.T)
-    weight = weight.reshape(-1, features)
 
     ids = jnp.arange(owners, dtype=jnp.int32)
     named = routes[:, :, None] == ids[None, None, :]
@@ -248,10 +262,19 @@
     packed = lax.dot_general(
         place, scaled, (((0,), (0,)), ((), ())), preferred_element_type=f32
     ).astype(bf16)
-    packed, grads_all, routes_all = lax.optimization_barrier((packed, grads_all, routes_all))
-    recv_act = lax.all_to_all(
-        packed.reshape(owners, rows, hidden), GROUP, split_axis=0, concat_axis=0, tiled=True
-    ).reshape(capacity, hidden)
+    packed = packed.reshape(owners, rows, hidden)
+    half, rest = hidden // 2, rows - tall
+    if folds:
+        low = packed[:, tall:]
+        low = jnp.concatenate([low[:, :, :half], low[:, :, half:]], axis=1)
+        packed = jnp.concatenate([packed[:, :tall], low], axis=2)
+    grads_all, weight, routes_all, recv_act = gather(out_grad, w_down[0], routes.T, packed)
+    weight = weight.reshape(-1, features)
+    if folds:
+        low = recv_act[:, :, hidden:]
+        low = jnp.concatenate([low[:, :rest], low[:, rest:]], axis=2)
+        recv_act = jnp.concatenate([recv_act[:, :, :hidden], low], axis=1)
+    recv_act = recv_act.reshape(capacity, hidden)
 
     mine = lax.axis_index(GROUP)
     has = jnp.any(routes_all == mine, axis=1)

time: 200 us -> 183 us (0.915)
  waiting for transfers between devices: 29.6 us -> 0.02 us
  Pallas kernels: 72.4 us -> 82.7 us
  blocking collectives: 47.3 us -> 55.2 us
  starting transfers between devices: 3.9 us -> 0.04 us
  matrix products: 26.3 us -> 22.7 us
    all_to_all x1 -> x0, waiting for transfers between devices: 29.6 us -> none  [local(): lax.all_to_all(packed.reshape(owners, rows, hidden), GROUP, split_axis=0,...]
    pallas_call x1, Pallas kernels: 72.4 us -> 82.7 us  [gather(): pl.pallas_call(functools.partial(gather_kernel, (n_dp, n_seq, n_expert, m...]
    all_to_all x1, blocking collectives: 47.3 us -> 55.2 us  [local(): lax.all_to_all(grad.reshape(owners, rows, hidden), GROUP, split_axis=0, c...]
    all_to_all x1 -> x0, starting transfers between devices: 3.85 us -> none  [local(): lax.all_to_all(packed.reshape(owners, rows, hidden), GROUP, split_axis=0,...]
    slice x0 -> x4, local copies, waits for them, and re-layouts: none -> 2.64 us  [the longest x1 1.35 us: local(): recv_act = jnp.concatenate([recv_act[:, :, :hidden], low], axis=1)]
    dot_general x1, matrix products: 7.98 us -> 5.71 us  [local(): lax.dot_general(recv_act, chosen, (((0,), (0,)), ((), ())), preferred_ele...]
    unnamed x10 -> x8, local copies, waits for them, and re-layouts: 3.58 us -> 1.47 us
  transfers between devices with their start and end apart: 2 -> 1, of which waited for: 1 -> 0; matrix products, arithmetic and copies ran while one was open for 7% -> 2% of each run, Pallas kernels for 0% -> 0%
where the time goes in v4:
time: 183 us
  Pallas kernels  82.7 us (45%)
  blocking collectives  55.2 us (30%)
  matrix products  22.7 us (12%)
  between operations  14.1 us (8%)
  local copies, waits for them, and re-layouts  4.48 us (2%)
  other arithmetic  3.69 us (2%)
    pallas_call x1, Pallas kernels, gather(): pl.pallas_call(functools.partial(gather_kernel, (n_dp, n_seq, n_expert, m...  82.7 us
    all_to_all x1, blocking collectives, local(): lax.all_to_all(grad.reshape(owners, rows, hidden), GROUP, split_axis=0, c...  55.2 us
    dot_general x1, matrix products, local(): lax.dot_general(recv_act, chosen, (((0,), (0,)), ((), ())), preferred_ele...  5.71 us
    dot_general x1, matrix products, local(): lax.dot_general(pick, grads_all, (((2,), (1,)), ((0,), (0,))), preferred_...  4.92 us
    dot_general x1, matrix products, local(): lax.dot_general(place, scaled, (((0,), (0,)), ((), ())), preferred_elemen...  4.13 us
    dot_general x1, matrix products, local(): lax.dot_general(chosen, weight, (((1,), (1,)), ((), ())), preferred_eleme...  3.89 us
    dot_general x1, matrix products, local(): home = jnp.dot(place, back, preferred_element_type=f32)  3.77 us
  transfers between devices with their start and end apart: 1, of which 0 were waited for; matrix products, arithmetic and copies ran while one was open for 2% of the time, Pallas kernels for 0%

profile of v4, /device:TPU:0, one launch (start us, length us, event | category | flops | bytes accessed | tf_op | source)
XLA Modules:
  0.0 182.9 jit_solution(5131060397093732937)
XLA Ops:
  7.2 0.0 reduce-scatter.2.cloned.1.call-start
  7.2 0.7 fusion.16
  7.9 0.1 fusion.15
  8.1 0.7 select_reduce_fusion
  8.8 0.7 convert_add_fusion
  9.5 0.1 copy.15
  9.6 0.1 eq.50
  9.7 0.8 copy.16
  10.5 0.1 mul.30
  10.6 4.1 %fusion.2 = bf16[1152,768]{1,0:T(8,128)(2,1)S(1)} fusion(s32[1024]{0:T(1024)S(1)} %eq.50, bf16[128,8,768]{2,1,0:T(8,128)(2,1)} %param.6, f32[1024]{0:T(1024)S(1)} %mul.30), kind=kOutput, calls=%fused_computation.6 | convolution fusion | flops 1816363008 | bytes 3350528 | tf_op jit(solution)/shard_map/dot_general | solution.py:262
  14.7 0.1 fusion.18
  14.8 0.1 slice.30
  14.8 1.4 maximum_maximum_fusion.packed
  16.3 82.7 %gather.1 = (bf16[16,128,2048]{2,1,0:T(8,128)(2,1)}, bf16[2,384,2048]{2,1,0:T(8,128)(2,1)}, s32[16,8,128]{2,1,0:T(8,128)}, bf16[16,48,1152]{2,1,0:T(8,128)(2,1)}) custom-call(bf16[128,2048]{1,0:T(8,128)(2,1)} %own.1, bf16[384,2048]{1,0:T(8,128)(2,1)} %bitcast.33, s32[8,128]{1,0:T(8,128)} %bitcast.34, bf16[16,48,1152]{2,1,0:T(8,128)(2,1)} %maximum_maximum_fusion.packed), custom_call_target="tpu_custom_call" | custom-call | tf_op jit(solution)/shard_map/gather/pallas_call | solution.py:204
  98.9 0.0 copy-start
  99.0 1.2 fusion.17
  100.1 1.3 slice.27
  101.5 0.0 copy-done
  101.5 0.1 convolution_convert_fusion.3
  101.7 0.0 copy-start.1
  101.7 4.9 %convolution_convert_fusion = bf16[16,72,2048]{2,1,0:T(8,128)(2,1)S(1)} fusion(bf16[16,128,2048]{2,1,0:T(8,128)(2,1)} %get-tuple-element.9, s32[16,128]{1,0:T(8,128)S(1)} %convolution_convert_fusion.3, pred[16,128]{1,0:T(8,128)(4,1)S(1)} %compare_reduce_fusion), kind=kOutput, calls=%fused_computation.3 | convolution fusion | flops 606633984 | bytes 13117440 | tf_op jit(solution)/shard_map/dot_general | solution.py:287
  106.6 0.0 copy-done.1
  106.6 3.9 %convolution_convert_fusion.2 = bf16[1152,768]{1,0:T(8,128)(2,1)S(1)} fusion(bf16[1152,2048]{1,0:T(8,128)(2,1)S(1)} %bitcast.26, bf16[768,2048]{1,0:T(8,128)(2,1)S(1)} %bitcast.35), kind=kOutput, calls=%fused_computation.8 | convolution fusion | flops 3624763392 | bytes 9633792 | tf_op jit(solution)/shard_map/dot_general | solution.py:291
  110.5 0.1 maximum_maximum_fusion.1
  110.6 5.7 %convolution_convert_fusion.1 = bf16[768,2048]{1,0:T(8,128)(2,1)} fusion(bf16[1152,768]{1,0:T(8,128)(2,1)S(1)} %bitcast.30, bf16[1152,2048]{1,0:T(8,128)(2,1)S(1)} %bitcast.27), kind=kOutput, calls=%fused_computation.7 | convolution fusion | flops 3625451520 | bytes 9633792 | tf_op jit(solution)/shard_map/dot_general | solution.py:298
  116.3 0.0 reduce-scatter.2.cloned.1.call-update
  116.4 0.0 copy-start.2
  116.4 55.2 %all_to_all.5 = bf16[16,72,768]{2,1,0:T(8,128)(2,1)S(1)} all-to-all(bf16[16,72,768]{2,1,0:T(8,128)(2,1)S(1)} %bitcast.28), channel_id=1, replica_groups=mesh['dp'=2,'seq'=2,'expert'=8] {'seq','expert'}, dimensions={0} | all-to-all | bytes 3538944 | tf_op jit(solution)/shard_map/all_to_all | solution.py:294
  171.6 0.0 copy-done.2
  171.6 3.8 %fusion.4 = (f32[1024]{0:T(1024)S(1)}, bf16[128,8,768]{2,1,0:T(8,128)(2,1)}) fusion(bf16[128,8,768]{2,1,0:T(8,128)(2,1)S(1)} %copy-done.2, f32[1024]{0:T(1024)S(1)} %mul.30, bf16[1152,768]{1,0:T(8,128)(2,1)S(1)} %bitcast.29, s32[1024]{0:T(1024)S(1)} %eq.50), kind=kOutput, calls=%fused_computation.10 | convolution fusion | flops 1817050112 | bytes 4927488 | tf_op jit(solution)/shard_map/dot_general | solution.py:304
  175.3 0.1 reshape.49
  175.4 0.7 copy.17
  (2 shorter events, 0.0 us)
Async XLA Ops:
  7.2 168.9 %reduce-scatter.2.cloned.1.call-start = ((), (), s32[]{:S(2)}) async-start(), calls=%async_computation.2 | async-start | bytes 4718592 | tf_op jit(solution)/shard_map/reduce_scatter | solution.py:301
  98.9 2.5 %copy-start = (s32[16,8,128]{2,1,0:T(8,128)S(1)}, s32[16,8,128]{2,1,0:T(8,128)}, u32[]{:S(2)}) copy-start(s32[16,8,128]{2,1,0:T(8,128)} %get-tuple-element.8) | copy-start | bytes 196612
  101.7 4.9 %copy-start.1 = (bf16[2,384,2048]{2,1,0:T(8,128)(2,1)S(1)}, bf16[2,384,2048]{2,1,0:T(8,128)(2,1)}, u32[]{:S(2)}) copy-start(bf16[2,384,2048]{2,1,0:T(8,128)(2,1)} %get-tuple-element.10) | copy-start | bytes 9437188
  116.4 55.2 %copy-start.2 = (bf16[128,8,768]{2,1,0:T(8,128)(2,1)S(1)}, bf16[128,8,768]{2,1,0:T(8,128)(2,1)}, u32[]{:S(2)}) copy-start(bf16[128,8,768]{2,1,0:T(8,128)(2,1)} %param.6) | copy-start | bytes 4718596
Sparse Core Ops, SparseCore 0:
  116.5 51.2 reduce-scatter.1

commit v5 on v4

--- a/solution.py
+++ b/solution.py
@@ -231,6 +231,64 @@
     )(out_grad, weight, named, packed)
 
 
+def exchange_kernel(sizes, blocks, arrived, here, send, recv):
+    n_seq, n_expert = sizes
+    n_group = n_seq * n_expert
+    dp, seq, expert = lax.axis_index("dp"), lax.axis_index("seq"), lax.axis_index("expert")
+    me = seq * n_expert + expert
+    barrier = pltpu.get_barrier_semaphore()
+
+    def member(i):
+        index = lax.rem(me + i, n_group)
+        return (dp, index // n_expert, lax.rem(index, n_expert))
+
+    def greet(i, _):
+        pl.semaphore_signal(
+            barrier, inc=1, device_id=member(i), device_id_type=pl.DeviceIdType.MESH
+        )
+
+    def push(source, target, i):
+        return pltpu.make_async_remote_copy(
+            src_ref=source,
+            dst_ref=target,
+            send_sem=send.at[i],
+            recv_sem=recv.at[i],
+            device_id=member(i),
+            device_id_type=pl.DeviceIdType.MESH,
+        )
+
+    def out(i):
+        return push(blocks.at[lax.rem(me + i, n_group)], arrived.at[me], i)
+
+    def finish(i, _):
+        block = arrived.at[lax.rem(me - i + n_group, n_group)]
+        push(block, block, i).wait_recv()
+        out(i).wait_send()
+
+    lax.fori_loop(1, n_group, greet, None)
+    pl.semaphore_wait(barrier, n_group - 1)
+    lax.fori_loop(1, n_group, lambda i, _: out(i).start(), None)
+    kept = pltpu.make_async_copy(blocks.at[me], arrived.at[me], here.at[0])
+    kept.start()
+    lax.fori_loop(1, n_group, finish, None)
+    kept.wait()
+
+
+def exchange(blocks):
+    n_seq, n_expert = lax.axis_size("seq"), lax.axis_size("expert")
+    sems = pltpu.SemaphoreType.DMA
+    hbm = pl.BlockSpec(memory_space=pl.ANY)
+    return pl.pallas_call(
+        functools.partial(exchange_kernel, (n_seq, n_expert)),
+        out_shape=jax.ShapeDtypeStruct(blocks.shape, blocks.dtype),
+        in_specs=[hbm],
+        out_specs=hbm,
+        scratch_shapes=[sems((1,)), sems((n_seq * n_expert,)), sems((n_seq * n_expert,))],
+        compiler_params=pltpu.CompilerParams(collective_id=1, has_side_effects=True),
+        name="exchange",
+    )(blocks)
+
+
 def local(out_grad, saved_act, gate_probs, routes, w_down):
     tokens, top = routes.shape
     hidden = saved_act.shape[2]
@@ -262,19 +320,28 @@
     packed = lax.dot_general(
         place, scaled, (((0,), (0,)), ((), ())), preferred_element_type=f32
     ).astype(bf16)
-    packed = packed.reshape(owners, rows, hidden)
     half, rest = hidden // 2, rows - tall
-    if folds:
-        low = packed[:, tall:]
+
+    def fold(array):
+        array = array.reshape(owners, rows, hidden)
+        if not folds:
+            return array
+        low = array[:, tall:]
         low = jnp.concatenate([low[:, :, :half], low[:, :, half:]], axis=1)
-        packed = jnp.concatenate([packed[:, :tall], low], axis=2)
-    grads_all, weight, routes_all, recv_act = gather(out_grad, w_down[0], routes.T, packed)
+        return jnp.concatenate([array[:, :tall], low], axis=2)
+
+    def unfold(array):
+        if folds:
+            low = array[:, :, hidden:]
+            low = jnp.concatenate([low[:, :rest], low[:, rest:]], axis=2)
+            array = jnp.concatenate([array[:, :, :hidden], low], axis=1)
+        return array.reshape(capacity, hidden)
+
+    grads_all, weight, routes_all, recv_act = gather(
+        out_grad, w_down[0], routes.T, fold(packed)
+    )
     weight = weight.reshape(-1, features)
-    if folds:
-        low = recv_act[:, :, hidden:]
-        low = jnp.concatenate([low[:, :rest], low[:, rest:]], axis=2)
-        recv_act = jnp.concatenate([recv_act[:, :, :hidden], low], axis=1)
-    recv_act = recv_act.reshape(capacity, hidden)
+    recv_act = unfold(recv_act)
 
     mine = lax.axis_index(GROUP)
     has = jnp.any(routes_all == mine, axis=1)
@@ -291,13 +358,11 @@
     grad = lax.dot_general(
         chosen, weight, (((1,), (1,)), ((), ())), preferred_element_type=f32
     ).astype(bf16)
-    back = lax.all_to_all(
-        grad.reshape(owners, rows, hidden), GROUP, split_axis=0, concat_axis=0, tiled=True
-    ).reshape(capacity, hidden)
-    recv_act, _ = lax.optimization_barrier((recv_act, grad))
     part = lax.dot_general(
         recv_act, chosen, (((0,), (0,)), ((), ())), preferred_element_type=f32
     ).astype(bf16)
+    grad, part = lax.optimization_barrier((grad, part))
+    back = unfold(exchange(fold(grad)))
     weight_grad = lax.psum_scatter(part, "dp", scatter_dimension=0, tiled=True).reshape(
         w_down.shape
     )

time: 183 us -> 182 us (level)
  the two profiles are of different devices: /device:TPU:0 before, /device:TPU:13 now
where the time goes in v5:
time: 182 us
  Pallas kernels  132 us (73%)
  matrix products  23.1 us (13%)
  between operations  14.2 us (8%)
  local copies, waits for them, and re-layouts  7.79 us (4%)
  other arithmetic  5.03 us (3%)
    pallas_call x1, Pallas kernels, gather(): pl.pallas_call(functools.partial(gather_kernel, (n_dp, n_seq, n_expert, m...  86.2 us
    pallas_call x1, Pallas kernels, exchange(): pl.pallas_call(functools.partial(exchange_kernel, (n_seq, n_expert)), out...  45.5 us
    dot_general x1, matrix products, local(): lax.dot_general(recv_act, chosen, (((0,), (0,)), ((), ())), preferred_ele...  6.17 us
    dot_general x1, matrix products, local(): lax.dot_general(pick, grads_all, (((2,), (1,)), ((0,), (0,))), preferred_...  4.92 us
    unnamed x10, local copies, waits for them, and re-layouts  4.2 us
    dot_general x1, matrix products, local(): lax.dot_general(place, scaled, (((0,), (0,)), ((), ())), preferred_elemen...  4.13 us
    dot_general x1, matrix products, local(): lax.dot_general(chosen, weight, (((1,), (1,)), ((), ())), preferred_eleme...  3.89 us
    dot_general x1, matrix products, local(): home = jnp.dot(place, back, preferred_element_type=f32)  3.75 us
  transfers between devices with their start and end apart: 1, of which 0 were waited for; matrix products, arithmetic and copies ran while one was open for 3% of the time, Pallas kernels for 25%

profile of v5, /device:TPU:13, one launch (start us, length us, event | category | flops | bytes accessed | tf_op | source)
XLA Modules:
  0.0 181.9 jit_solution(10400729154447326497)
XLA Ops:
  7.2 0.0 reduce-scatter.2.cloned.1.call-start
  7.2 0.7 fusion.21
  7.9 0.1 fusion.20
  8.1 0.7 select_reduce_fusion
  8.8 0.7 convert_add_fusion
  9.5 0.1 copy.15
  9.6 0.1 eq.50
  9.7 0.8 copy.16
  10.5 0.1 mul.30
  10.6 4.1 %fusion.2 = bf16[1152,768]{1,0:T(8,128)(2,1)S(1)} fusion(s32[1024]{0:T(1024)S(1)} %eq.50, bf16[128,8,768]{2,1,0:T(8,128)(2,1)} %param.6, f32[1024]{0:T(1024)S(1)} %mul.30), kind=kOutput, calls=%fused_computation.7 | convolution fusion | flops 1816363008 | bytes 3350528 | tf_op jit(solution)/shard_map/dot_general | solution.py:320
  14.7 0.1 fusion.26
  14.8 0.1 slice.60
  14.8 1.4 maximum_maximum_fusion.packed
  16.2 86.2 %gather.1 = (bf16[16,128,2048]{2,1,0:T(8,128)(2,1)}, bf16[2,384,2048]{2,1,0:T(8,128)(2,1)}, s32[16,8,128]{2,1,0:T(8,128)}, bf16[16,48,1152]{2,1,0:T(8,128)(2,1)}) custom-call(bf16[128,2048]{1,0:T(8,128)(2,1)} %own.1, bf16[384,2048]{1,0:T(8,128)(2,1)} %bitcast.32, s32[8,128]{1,0:T(8,128)} %bitcast.33, bf16[16,48,1152]{2,1,0:T(8,128)(2,1)} %maximum_maximum_fusion.packed), custom_call_target="tpu_custom_call" | custom-call | tf_op jit(solution)/shard_map/gather/pallas_call | solution.py:204
  102.5 1.2 fusion.25
  103.7 1.3 slice.51
  105.1 0.1 convolution_convert_fusion.2
  105.2 4.9 %convolution_convert_fusion = bf16[16,72,2048]{2,1,0:T(8,128)(2,1)S(1)} fusion(bf16[16,128,2048]{2,1,0:T(8,128)(2,1)} %get-tuple-element.10, s32[16,128]{1,0:T(8,128)S(1)} %convolution_convert_fusion.2, pred[16,128]{1,0:T(8,128)(4,1)S(1)} %compare_reduce_fusion), kind=kOutput, calls=%fused_computation.4 | convolution fusion | flops 606633984 | bytes 13117440 | tf_op jit(solution)/shard_map/dot_general | solution.py:354
  110.1 3.9 %convolution_convert_fusion.1 = bf16[1152,768]{1,0:T(8,128)(2,1)S(1)} fusion(bf16[1152,2048]{1,0:T(8,128)(2,1)S(1)} %bitcast.26, bf16[768,2048]{1,0:T(8,128)(2,1)S(1)} %bitcast.34), kind=kOutput, calls=%fused_computation.8 | convolution fusion | flops 3624763392 | bytes 9633792 | tf_op jit(solution)/shard_map/dot_general | solution.py:358
  114.0 6.2 %bitcast_convert_fusion = bf16[768,2048]{1,0:T(8,128)(2,1)} fusion(bf16[16,72,2048]{2,1,0:T(8,128)(2,1)S(1)} %convolution_convert_fusion, bf16[16,24,384]{2,1,0:T(8,128)(2,1)S(1)} %get-tuple-element.28, bf16[16,24,384]{2,1,0:T(8,128)(2,1)S(1)} %get-tuple-element.27, bf16[16,48,768]{2,1,0:T(8,128)(2,1)S(1)} %slice.51), kind=kOutput, calls=%fused_computation | convolution fusion | flops 3630759936 | bytes 9633792 | tf_op jit(solution)/shard_map/dot_general | solution.py:361
  120.2 0.1 slice.63
  120.3 0.1 fusion.24
  120.4 1.3 maximum_maximum_fusion.1.blocks
  121.7 45.5 %exchange.1 = bf16[16,48,1152]{2,1,0:T(8,128)(2,1)} custom-call(bf16[16,48,1152]{2,1,0:T(8,128)(2,1)} %maximum_maximum_fusion.1.blocks), custom_call_target="tpu_custom_call" | custom-call | tf_op jit(solution)/shard_map/exchange/pallas_call | solution.py:281
  167.3 1.5 copy-done
  168.7 0.1 fusion.23
  168.8 0.4 slice-done
  169.2 0.1 maximum_maximum_fusion.2
  169.3 1.3 copy-done.3
  170.6 3.7 %fusion.4 = (f32[1024]{0:T(1024)S(1)}, bf16[128,8,768]{2,1,0:T(8,128)(2,1)}) fusion(bf16[128,8,768]{2,1,0:T(8,128)(2,1)S(1)} %copy-done.3, f32[1024]{0:T(1024)S(1)} %mul.30, bf16[1152,768]{1,0:T(8,128)(2,1)S(1)} %bitcast.27, s32[1024]{0:T(1024)S(1)} %eq.50), kind=kOutput, calls=%fused_computation.10 | convolution fusion | flops 1817050112 | bytes 4927488 | tf_op jit(solution)/shard_map/dot_general | solution.py:369
  174.3 0.1 reshape.47
  174.4 0.7 copy.17
  (10 shorter events, 0.1 us)
Async XLA Ops:
  7.2 167.9 %reduce-scatter.2.cloned.1.call-start = ((), (), s32[]{:S(2)}) async-start(), calls=%async_computation.1 | async-start | bytes 4718592 | tf_op jit(solution)/shard_map/reduce_scatter | solution.py:366
  102.5 2.5 %copy-start.1 = (s32[16,8,128]{2,1,0:T(8,128)S(1)}, s32[16,8,128]{2,1,0:T(8,128)}, u32[]{:S(2)}) copy-start(s32[16,8,128]{2,1,0:T(8,128)} %get-tuple-element.9) | copy-start | bytes 196612
  105.2 4.9 %copy-start.2 = (bf16[2,384,2048]{2,1,0:T(8,128)(2,1)S(1)}, bf16[2,384,2048]{2,1,0:T(8,128)(2,1)}, u32[]{:S(2)}) copy-start(bf16[2,384,2048]{2,1,0:T(8,128)(2,1)} %get-tuple-element.11) | copy-start | bytes 9437188
  167.2 1.5 copy-start
  167.2 1.9 %slice-start = ((bf16[16,48,1152]{2,1,0:T(8,128)(2,1)}), bf16[16,48,768]{2,1,0:T(8,128)(2,1)S(1)}, s32[]{:S(2)}) async-start(bf16[16,48,1152]{2,1,0:T(8,128)(2,1)} %exchange.1), calls=%async_computation.2 | async-start | bytes 2359296 | tf_op jit(solution)/shard_map/slice | solution.py:337
  169.2 1.4 copy-start.3
Sparse Core Ops, SparseCore 0:
  120.4 46.0 reduce-scatter.1

commit v6 on v5

--- a/solution.py
+++ b/solution.py
@@ -172,7 +172,8 @@
         for test, zb in waiting:
             arrive_y(test, zb)
         waiting = fresh
-    lax.fori_loop(1, n_group, lambda i, _: a_copy(i).start(), None)
+        if hop == max(1, lines - 2):
+            lax.fori_loop(1, n_group, lambda i, _: a_copy(i).start(), None)
     for test, zb in waiting:
         arrive_y(test, zb)
     for i in range(1, n_seq):

time: 182 us -> 171 us (0.940)
  the two profiles are of different devices: /device:TPU:13 before, /device:TPU:15 now
where the time goes in v6:
time: 171 us
  Pallas kernels  121 us (71%)
  matrix products  23.1 us (14%)
  between operations  14.2 us (8%)
  local copies, waits for them, and re-layouts  7.79 us (5%)
  other arithmetic  5.03 us (3%)
    pallas_call x1, Pallas kernels, gather(): pl.pallas_call(functools.partial(gather_kernel, (n_dp, n_seq, n_expert, m...  73.9 us
    pallas_call x1, Pallas kernels, exchange(): pl.pallas_call(functools.partial(exchange_kernel, (n_seq, n_expert)), out...  46.7 us
    dot_general x1, matrix products, local(): lax.dot_general(recv_act, chosen, (((0,), (0,)), ((), ())), preferred_ele...  6.17 us
    dot_general x1, matrix products, local(): lax.dot_general(pick, grads_all, (((2,), (1,)), ((0,), (0,))), preferred_...  4.92 us
    unnamed x10, local copies, waits for them, and re-layouts  4.2 us
    dot_general x1, matrix products, local(): lax.dot_general(place, scaled, (((0,), (0,)), ((), ())), preferred_elemen...  4.13 us
    dot_general x1, matrix products, local(): lax.dot_general(chosen, weight, (((1,), (1,)), ((), ())), preferred_eleme...  3.89 us
    dot_general x1, matrix products, local(): home = jnp.dot(place, back, preferred_element_type=f32)  3.75 us
  transfers between devices with their start and end apart: 1, of which 0 were waited for; matrix products, arithmetic and copies ran while one was open for 4% of the time, Pallas kernels for 27%

profile of v6, /device:TPU:15, one launch (start us, length us, event | category | flops | bytes accessed | tf_op | source)
XLA Modules:
  0.0 170.7 jit_solution(8455824861060223322)
XLA Ops:
  7.2 0.0 reduce-scatter.2.cloned.1.call-start
  7.2 0.7 fusion.21
  7.9 0.1 fusion.20
  8.1 0.7 select_reduce_fusion
  8.8 0.7 convert_add_fusion
  9.5 0.1 copy.15
  9.6 0.1 eq.50
  9.7 0.8 copy.16
  10.5 0.1 mul.30
  10.6 4.1 %fusion.2 = bf16[1152,768]{1,0:T(8,128)(2,1)S(1)} fusion(s32[1024]{0:T(1024)S(1)} %eq.50, bf16[128,8,768]{2,1,0:T(8,128)(2,1)} %param.6, f32[1024]{0:T(1024)S(1)} %mul.30), kind=kOutput, calls=%fused_computation.7 | convolution fusion | flops 1816363008 | bytes 3350528 | tf_op jit(solution)/shard_map/dot_general | solution.py:321
  14.7 0.1 fusion.26
  14.8 0.1 slice.60
  14.8 1.4 maximum_maximum_fusion.packed
  16.3 73.9 %gather.1 = (bf16[16,128,2048]{2,1,0:T(8,128)(2,1)}, bf16[2,384,2048]{2,1,0:T(8,128)(2,1)}, s32[16,8,128]{2,1,0:T(8,128)}, bf16[16,48,1152]{2,1,0:T(8,128)(2,1)}) custom-call(bf16[128,2048]{1,0:T(8,128)(2,1)} %own.1, bf16[384,2048]{1,0:T(8,128)(2,1)} %bitcast.32, s32[8,128]{1,0:T(8,128)} %bitcast.33, bf16[16,48,1152]{2,1,0:T(8,128)(2,1)} %maximum_maximum_fusion.packed), custom_call_target="tpu_custom_call" | custom-call | tf_op jit(solution)/shard_map/gather/pallas_call | solution.py:205
  90.1 1.2 fusion.25
  91.3 1.3 slice.51
  92.7 0.1 convolution_convert_fusion.2
  92.8 4.9 %convolution_convert_fusion = bf16[16,72,2048]{2,1,0:T(8,128)(2,1)S(1)} fusion(bf16[16,128,2048]{2,1,0:T(8,128)(2,1)} %get-tuple-element.10, s32[16,128]{1,0:T(8,128)S(1)} %convolution_convert_fusion.2, pred[16,128]{1,0:T(8,128)(4,1)S(1)} %compare_reduce_fusion), kind=kOutput, calls=%fused_computation.4 | convolution fusion | flops 606633984 | bytes 13117440 | tf_op jit(solution)/shard_map/dot_general | solution.py:355
  97.8 3.9 %convolution_convert_fusion.1 = bf16[1152,768]{1,0:T(8,128)(2,1)S(1)} fusion(bf16[1152,2048]{1,0:T(8,128)(2,1)S(1)} %bitcast.26, bf16[768,2048]{1,0:T(8,128)(2,1)S(1)} %bitcast.34), kind=kOutput, calls=%fused_computation.8 | convolution fusion | flops 3624763392 | bytes 9633792 | tf_op jit(solution)/shard_map/dot_general | solution.py:359
  101.7 6.2 %bitcast_convert_fusion = bf16[768,2048]{1,0:T(8,128)(2,1)} fusion(bf16[16,72,2048]{2,1,0:T(8,128)(2,1)S(1)} %convolution_convert_fusion, bf16[16,24,384]{2,1,0:T(8,128)(2,1)S(1)} %get-tuple-element.28, bf16[16,24,384]{2,1,0:T(8,128)(2,1)S(1)} %get-tuple-element.27, bf16[16,48,768]{2,1,0:T(8,128)(2,1)S(1)} %slice.51), kind=kOutput, calls=%fused_computation | convolution fusion | flops 3630759936 | bytes 9633792 | tf_op jit(solution)/shard_map/dot_general | solution.py:362
  107.9 0.1 slice.63
  108.0 0.1 fusion.24
  108.0 1.3 maximum_maximum_fusion.1.blocks
  109.4 46.7 %exchange.1 = bf16[16,48,1152]{2,1,0:T(8,128)(2,1)} custom-call(bf16[16,48,1152]{2,1,0:T(8,128)(2,1)} %maximum_maximum_fusion.1.blocks), custom_call_target="tpu_custom_call" | custom-call | tf_op jit(solution)/shard_map/exchange/pallas_call | solution.py:282
  156.1 1.5 copy-done
  157.5 0.1 fusion.23
  157.6 0.4 slice-done
  158.0 0.1 maximum_maximum_fusion.2
  158.1 1.3 copy-done.3
  159.4 3.8 %fusion.4 = (f32[1024]{0:T(1024)S(1)}, bf16[128,8,768]{2,1,0:T(8,128)(2,1)}) fusion(bf16[128,8,768]{2,1,0:T(8,128)(2,1)S(1)} %copy-done.3, f32[1024]{0:T(1024)S(1)} %mul.30, bf16[1152,768]{1,0:T(8,128)(2,1)S(1)} %bitcast.27, s32[1024]{0:T(1024)S(1)} %eq.50), kind=kOutput, calls=%fused_computation.10 | convolution fusion | flops 1817050112 | bytes 4927488 | tf_op jit(solution)/shard_map/dot_general | solution.py:370
  163.2 0.1 reshape.47
  163.2 0.7 copy.17
  (10 shorter events, 0.1 us)
Async XLA Ops:
  7.2 156.7 %reduce-scatter.2.cloned.1.call-start = ((), (), s32[]{:S(2)}) async-start(), calls=%async_computation.1 | async-start | bytes 4718592 | tf_op jit(solution)/shard_map/reduce_scatter | solution.py:367
  90.1 2.5 %copy-start.1 = (s32[16,8,128]{2,1,0:T(8,128)S(1)}, s32[16,8,128]{2,1,0:T(8,128)}, u32[]{:S(2)}) copy-start(s32[16,8,128]{2,1,0:T(8,128)} %get-tuple-element.9) | copy-start | bytes 196612
  92.8 4.9 %copy-start.2 = (bf16[2,384,2048]{2,1,0:T(8,128)(2,1)S(1)}, bf16[2,384,2048]{2,1,0:T(8,128)(2,1)}, u32[]{:S(2)}) copy-start(bf16[2,384,2048]{2,1,0:T(8,128)(2,1)} %get-tuple-element.11) | copy-start | bytes 9437188
  156.1 1.5 copy-start
  156.1 1.9 %slice-start = ((bf16[16,48,1152]{2,1,0:T(8,128)(2,1)}), bf16[16,48,768]{2,1,0:T(8,128)(2,1)S(1)}, s32[]{:S(2)}) async-start(bf16[16,48,1152]{2,1,0:T(8,128)(2,1)} %exchange.1), calls=%async_computation.2 | async-start | bytes 2359296 | tf_op jit(solution)/shard_map/slice | solution.py:338
  158.0 1.4 copy-start.3
Sparse Core Ops, SparseCore 0:
  108.0 46.3 reduce-scatter.1
